TPU v7x, 32 devices: a whole 2x2x4 slice. The times are simulated.
32 devices in a mesh: group: 16 (over z, y, core), tp: 2 (over x).
Axes of the slice: x: 2, y: 2, z: 4, core: 2. Of those that a mesh axis runs over, the one named last changes fastest.
Arguments:
- queries: bfloat16 [1024, 2048], P('group', 'tp'), may hold values from -22 to 22
- new_kv: bfloat16 [1024, 1024], P('group', 'tp'), may hold values from -6 to 6
- local_cache: bfloat16 [4096, 1024], P('group', 'tp'), may hold values from -6 to 6
- remote_pool: bfloat16 [2048, 1024], P('group', 'tp'), may hold values from -6 to 6
- page_index: int32 [16, 16], P('group'), may hold values from 0 to 15, each once within a row
- lengths: int32 [16], P('group'), may hold values from 256 to 384, as said below
- sinks: float32 [32], P('tp'), may hold values from 4 to 8
- out_weight: bfloat16 [2048, 2880], P('tp'), may hold values from -0.125 to 0.125
- residual: bfloat16 [1024, 2880], P('group', 'tp'), may hold values from -6 to 6
- norm_gain: float32 [2880], replicated, may hold values from 0.5 to 2
- routes: int32 [1024, 4], P('group'), may hold values from 0 to 7, all different within a row; in each aligned block of 64 rows (0 to 63, 64 to 127, ...) at most 40 rows name the same one
- route_weights: float32 [1024, 4], P('group'), may hold values from 0.1 to 1
- expert_gate: bfloat16 [16, 2880, 1440], P('group', None, 'tp'), may hold values from -0.109375 to 0.109375
- expert_up: bfloat16 [16, 2880, 1440], P('group', None, 'tp'), may hold values from -0.109375 to 0.109375
- expert_down: bfloat16 [16, 1440, 2880], P('group', None, 'tp'), may hold values from -0.109375 to 0.109375
Outputs:
- layer_out: bfloat16 [1024, 2880], P('group', 'tp')
Inputs may be any that keep to these rules, and one draw needn't show every extreme that they name: `lengths`: every request has at least 256 cached positions; some request has exactly 256, some exactly 384. `routes`: within the rows of one request no expert is named by more than 40 rows. `page_index`: each row is a permutation.
All inputs are finite; a program needn't handle non-finite values.
Results may differ from a plain program's by a relative error of at most 0.013.
Values may be sent and summed in bfloat16 or wider, within the bound.
No kernel may reach another device: no remote copies, remote signals or barrier semaphores. Data moves between devices by JAX's collectives and lax.ppermute only.
A program may use at most 128 MiB of HBM per device.

v0:
```python
import functools

import jax
import jax.numpy as jnp
from jax import lax
from jax.experimental import pallas as pl
from jax.experimental.pallas import tpu as pltpu
from jax.sharding import PartitionSpec as P

HEAD = 64
TILE = 256
PARTS = 1
VMEM_LIMIT = 24 * 1024 * 1024


THETA = 150000.0
ALPHA = 1.702
EPSILON = 1e-05


def exchange(value, axis, offset):
    if offset == 0:
        return value
    size = lax.axis_size(axis)
    return lax.ppermute(value, axis, [(i, i ^ offset) for i in range(size)])


NT = (((1,), (1,)), ((), ()))


def dot_nt(left, right):
    return lax.dot_general(left, right, NT, preferred_element_type=jnp.float32)


def swapped_halves(value):
    lanes = value.shape[1]
    lane = lax.broadcasted_iota(jnp.int32, value.shape, 1)
    return jnp.where(
        lane % HEAD < HEAD // 2,
        pltpu.roll(value, lanes - HEAD // 2, 1),
        pltpu.roll(value, HEAD // 2, 1),
    )


def local_kernel(sink_ref, query_ref, kv_ref, local_ref, cos_ref, sin_ref, rotated_ref, state_ref):
    tokens = query_ref.shape[0]
    pair = 2 * HEAD
    kv_heads = kv_ref.shape[1] // pair
    group_size = query_ref.shape[1] // HEAD // kv_heads
    rows = group_size * tokens
    cosine, sine = cos_ref[...], sin_ref[...]
    low = lax.broadcasted_iota(jnp.int32, (tokens, pair), 1) < HEAD
    lane = lax.broadcasted_iota(jnp.int32, (rows, pair), 1)

    def rotated(value):
        return value * cosine + swapped_halves(value) * sine

    token_row = lax.broadcasted_iota(jnp.int32, (rows, tokens), 0) % tokens
    causal = lax.broadcasted_iota(jnp.int32, (rows, tokens), 1) <= token_row
    for h in range(kv_heads):
        lanes = slice(h * pair, (h + 1) * pair)
        own = kv_ref[:, lanes]
        own = jnp.where(low, rotated(own.astype(jnp.float32)).astype(jnp.bfloat16), own)
        queries = []
        for i in range(group_size // 2):
            start = (h * group_size + 2 * i) * HEAD
            both = rotated(query_ref[:, start : start + pair].astype(jnp.float32)) * HEAD**-0.5
            queries.append(jnp.where(low, both, 0.0))
            queries.append(jnp.where(low, pltpu.roll(both, HEAD, 1), 0.0))
        query = jnp.concatenate(queries, axis=0).astype(jnp.bfloat16)
        sink = jnp.concatenate(
            [jnp.full((tokens, 1), sink_ref[h * group_size + i]) for i in range(group_size)], axis=0
        )
        sources = [local_ref[:, lanes], own]
        scores = [dot_nt(query, source) for source in sources]
        scores[1] = jnp.where(causal, scores[1], -jnp.inf)
        row_max = sink
        for score in scores:
            row_max = jnp.maximum(row_max, jnp.max(score, axis=1, keepdims=True))
        denominator = jnp.exp(sink - row_max)
        blended = None
        for score, source in zip(scores, sources):
            weights = jnp.exp(score - row_max)
            denominator = denominator + jnp.sum(weights, axis=1, keepdims=True)
            term = jnp.dot(weights.astype(jnp.bfloat16), source, preferred_element_type=jnp.float32)
            blended = term if blended is None else blended + term
        place = slice(h * rows, (h + 1) * rows)
        rotated_ref[place, :] = query
        state_ref[place, :] = jnp.where(lane == 0, row_max, jnp.where(lane == 1, denominator, blended))


def split_copies(source, target, sems, first, parts):
    rows = source.shape[0]
    step = rows if parts == 1 else -(-rows // parts) // 16 * 16 + 16
    return [
        pltpu.make_async_copy(
            source.at[start : min(start + step, rows)],
            target.at[start : min(start + step, rows)],
            sems.at[first + i],
        )
        for i, start in enumerate(range(0, rows, step))
    ]


def start_all(copies):
    for copy in copies:
        copy.start()


def wait_all(copies):
    for copy in copies:
        copy.wait()


def page_kernel(me_ref, weight_ref, rotated_ref, state_ref, page_ref, valid_ref, attended_ref, *refs):
    other_refs, held_ref, sems = refs[:-2], refs[-2], refs[-1]
    copies = [
        split_copies(weight_ref.at[me_ref[0] ^ (j + 1)], held_ref.at[j], sems, PARTS * j, PARTS)
        for j in range(len(other_refs))
    ]
    for some in copies:
        start_all(some)
    tokens = attended_ref.shape[0]
    pair = 2 * HEAD
    kv_heads = page_ref.shape[1] // pair
    rows = rotated_ref.shape[0] // kv_heads
    group_size = rows // tokens
    low = lax.broadcasted_iota(jnp.int32, (tokens, pair), 1) < HEAD
    page_valid = valid_ref[...] > 0.0
    for h in range(kv_heads):
        place = slice(h * rows, (h + 1) * rows)
        source = page_ref[:, h * pair : (h + 1) * pair]
        state = state_ref[place, :]
        score = jnp.where(page_valid, dot_nt(rotated_ref[place, :], source), -jnp.inf)
        row_max = jnp.maximum(state[:, 0:1], jnp.max(score, axis=1, keepdims=True))
        weights = jnp.exp(score - row_max)
        kept = jnp.exp(state[:, 0:1] - row_max)
        denominator = state[:, 1:2] * kept + jnp.sum(weights, axis=1, keepdims=True)
        term = jnp.dot(weights.astype(jnp.bfloat16), source, preferred_element_type=jnp.float32)
        blended = (state * kept + term) / denominator
        for i in range(group_size // 2):
            even = blended[2 * i * tokens : (2 * i + 1) * tokens]
            odd = blended[(2 * i + 1) * tokens : (2 * i + 2) * tokens]
            start = (h * group_size + 2 * i) * HEAD
            attended_ref[:, start : start + pair] = jnp.where(
                low, pltpu.roll(even, HEAD, 1), odd
            ).astype(jnp.bfloat16)
    attended = attended_ref[...]
    for j, ref in enumerate(other_refs):
        wait_all(copies[j])
        ref[...] = dot_nt(attended, held_ref[j]).astype(jnp.bfloat16)


def own_columns_kernel(
    me_ref, weight_ref, residual_ref, attended_ref, out_ref, sent_ref, held_ref, rows_ref, sems
):
    copies = split_copies(weight_ref.at[me_ref[0]], held_ref, sems, 0, PARTS)
    copies.append(pltpu.make_async_copy(residual_ref, rows_ref, sems.at[PARTS]))
    start_all(copies)
    wait_all(copies)
    terms = rows_ref[...].astype(jnp.float32) + dot_nt(attended_ref[...], held_ref[...])
    out_ref[...] = terms
    sent_ref[...] = terms.astype(jnp.bfloat16)


def tiles(size):
    return [slice(start, min(start + TILE, size)) for start in range(0, size, TILE)]


def gate_up_kernel(parts, me_ref, gate_ref, up_ref, gain_ref, *refs):
    sets, (out_ref, place_ref, row_ref, gate_held, up_held, gain_held, sems) = refs[:-7], refs[-7:]
    rows, width = sets[0].shape[1:]
    features, hidden = gate_ref.shape[1], gate_ref.shape[0]
    gain_copy = pltpu.make_async_copy(gain_ref, gain_held, sems.at[0])
    gain_copy.start()
    copies = []
    for t, tile in enumerate(tiles(hidden)):
        some = split_copies(gate_ref.at[tile], gate_held.at[tile], sems, 1 + 4 * t, 2)
        some += split_copies(up_ref.at[tile], up_held.at[tile], sems, 3 + 4 * t, 2)
        start_all(some)
        copies.append(some)
    me = me_ref[0]
    gain_copy.wait()
    for s, ref in enumerate(sets):
        held = [ref[j].astype(jnp.float32) for j in range(parts)]
        square = sum(jnp.sum(h * h, axis=1, keepdims=True) for h in held)
        scale = lax.rsqrt(square / features + EPSILON)
        for j in range(parts):
            place_ref[me ^ j] = held[j] * scale
        whole = jnp.concatenate([place_ref[p] for p in range(parts)], axis=1)
        row_ref[pl.ds(s * rows, rows), :] = (whole * gain_held[...]).astype(jnp.bfloat16)
    for t, tile in enumerate(tiles(hidden)):
        wait_all(copies[t])
        gate_val = dot_nt(row_ref[...], gate_held[tile])
        up_val = dot_nt(row_ref[...], up_held[tile])
        active = gate_val * jax.nn.sigmoid(ALPHA * gate_val) * (up_val + 1.0)
        out_ref[:, tile] = active.astype(jnp.bfloat16)


def down_kernel(me_ref, down_ref, *refs):
    own_ref, other_ref, held_ref, total_ref, sems = refs[-5:]
    actives = refs[:-5]
    rows, width = own_ref.shape
    copies = [
        split_copies(down_ref.at[me_ref[0] ^ j], held_ref.at[j], sems, PARTS * j, PARTS)
        for j in range(len(actives))
    ]
    for some in copies:
        start_all(some)
    for j, ref in enumerate(actives):
        wait_all(copies[j])
        for tile in tiles(width):
            term = jnp.dot(ref[...], held_ref[j, :, tile], preferred_element_type=jnp.float32)
            if j > 0:
                term = term + total_ref[:, tile]
            if j < len(actives) - 1:
                total_ref[:, tile] = term
            else:
                own_ref[:, tile] = term[:rows].astype(jnp.bfloat16)
                other_ref[:, tile] = term[rows:].astype(jnp.bfloat16)


def kernel_call(kernel, out_types, scalars, sources, *operands, scratch=()):
    in_vmem = pl.BlockSpec(memory_space=pltpu.VMEM)
    in_hbm = pl.BlockSpec(memory_space=pltpu.HBM)
    return pl.pallas_call(
        kernel,
        out_shape=[pltpu.VMEM(shape, dtype) for shape, dtype in out_types],
        in_specs=[pl.BlockSpec(memory_space=pltpu.SMEM)] * len(scalars)
        + [in_hbm] * len(sources)
        + [in_vmem] * len(operands),
        out_specs=[in_vmem] * len(out_types),
        scratch_shapes=scratch,
        compiler_params=pltpu.CompilerParams(vmem_limit_bytes=VMEM_LIMIT),
    )(
        *scalars,
        *[pltpu.with_memory_space_constraint(value, pltpu.HBM) for value in sources],
        *[pltpu.with_memory_space_constraint(value, pltpu.VMEM) for value in operands],
    )


def on_device(
    queries,
    new_kv,
    local_cache,
    remote_pool,
    page_index,
    lengths,
    sinks,
    out_weight,
    residual,
    norm_gain,
    routes,
    route_weights,
    expert_gate,
    expert_up,
    expert_down,
):
    groups = lax.axis_size("group")
    tp = lax.axis_size("tp")
    me_tp = lax.axis_index("tp")
    experts = groups // 2
    me_expert = lax.axis_index("group") // 2
    tp_scalar = me_tp.astype(jnp.int32).reshape(1)
    lane_count = remote_pool.shape[1]
    local_len = local_cache.shape[0]
    fetched = lax.all_to_all(
        remote_pool.reshape(groups, -1, lane_count),
        "group",
        split_axis=0,
        concat_axis=0,
        tiled=True,
    )
    page_len = fetched.shape[1]
    length = lengths[0]
    offsets = jnp.arange(page_len, dtype=jnp.int32)
    remote_pos = local_len + page_index[0][:, None] * page_len + offsets[None, :]
    page_valid = (remote_pos < length).astype(jnp.float32).reshape(1, -1)
    block_len, width = residual.shape
    positions = (length + jnp.arange(block_len, dtype=jnp.int32)).astype(jnp.float32)
    lane = jnp.arange(2 * HEAD, dtype=jnp.int32) % HEAD
    inverse = THETA ** (-2.0 * (lane % (HEAD // 2)).astype(jnp.float32) / HEAD)
    angles = positions[:, None] * inverse[None, :]
    sine = jnp.where(lane < HEAD // 2, -1.0, 1.0)[None, :] * jnp.sin(angles)
    hidden = expert_gate.shape[2]
    weight = out_weight.T.reshape(tp, width, out_weight.shape[0])
    gate, up = expert_gate[0].T, expert_up[0].T
    down = expert_down.reshape(tp, hidden, width)
    gain = norm_gain.reshape(1, tp * width)
    dma = pltpu.SemaphoreType.DMA
    in_vmem = pl.BlockSpec(memory_space=pltpu.VMEM)
    states = block_len * queries.shape[1] // HEAD
    rotated, state = pl.pallas_call(
        local_kernel,
        out_shape=[
            pltpu.VMEM((states, 2 * HEAD), jnp.bfloat16),
            pltpu.VMEM((states, 2 * HEAD), jnp.float32),
        ],
        in_specs=[pl.BlockSpec(memory_space=pltpu.SMEM)] + [in_vmem] * 5,
        out_specs=[in_vmem] * 2,
        compiler_params=pltpu.CompilerParams(vmem_limit_bytes=VMEM_LIMIT),
    )(
        sinks,
        *[pltpu.with_memory_space_constraint(value, pltpu.HBM) for value in (queries, new_kv, local_cache)],
        *[pltpu.with_memory_space_constraint(value, pltpu.VMEM) for value in (jnp.cos(angles), sine)],
    )
    attended, *others = kernel_call(
        page_kernel,
        [(queries.shape, jnp.bfloat16)] + [(residual.shape, jnp.bfloat16)] * (tp - 1),
        [tp_scalar],
        [weight],
        rotated,
        state,
        fetched.reshape(-1, lane_count),
        page_valid,
        scratch=[pltpu.VMEM((tp - 1, *weight.shape[1:]), jnp.bfloat16), dma((PARTS * (tp - 1),))],
    )
    arriving = [exchange(other, "tp", j + 1) for j, other in enumerate(others)]
    own_state, own_terms = kernel_call(
        own_columns_kernel,
        [(residual.shape, jnp.float32), (residual.shape, jnp.bfloat16)],
        [tp_scalar],
        [weight, residual],
        lax.optimization_barrier((attended, gain))[0],
        scratch=[
            pltpu.VMEM(weight.shape[1:], jnp.bfloat16),
            pltpu.VMEM(residual.shape, jnp.bfloat16),
            dma((PARTS + 1,)),
        ],
    )
    for term in arriving:
        own_state = own_state + term.astype(jnp.float32)
    state_sent = own_state.astype(jnp.bfloat16)
    if tp == 2:
        own_terms = lax.optimization_barrier((own_terms, state_sent))[0]
        other_state = exchange(own_terms, "tp", 1).astype(jnp.float32) + others[0].astype(jnp.float32)
        own_blocks = [state_sent, other_state.astype(jnp.bfloat16)]
    else:
        own_blocks = [exchange(state_sent, "tp", j) for j in range(tp)]

    top_count = routes.shape[1]
    capacity = 5 * block_len * top_count // (4 * experts)
    half = experts // 2
    mixing = route_weights / jnp.sum(route_weights, axis=1, keepdims=True)
    plan = jnp.concatenate([routes.astype(jnp.float32), mixing], axis=1)
    far_plan = exchange(lax.optimization_barrier((plan, own_blocks[-1]))[0], "group", experts)

    def slots(chosen_experts, weights):
        chosen = (chosen_experts ^ me_expert)[:, :, None] == jnp.arange(half, dtype=jnp.int32)
        member = jnp.any(chosen, axis=1)
        mix = jnp.sum(jnp.where(chosen, weights[:, :, None], 0.0), axis=1)
        earlier = jnp.arange(block_len)[:, None] > jnp.arange(block_len)[None, :]
        rank = jnp.dot(
            earlier.astype(jnp.bfloat16), member.astype(jnp.bfloat16), preferred_element_type=jnp.float32
        ).astype(jnp.int32)
        hit = member.T[:, None, :] & (
            rank.T[:, None, :] == jnp.arange(capacity, dtype=jnp.int32)[None, :, None]
        )
        pick = hit.astype(jnp.bfloat16).reshape(half * capacity, block_len)
        spread = jnp.where(hit, mix.T[:, None, :], 0.0).reshape(half * capacity, block_len)
        high = spread.astype(jnp.bfloat16)
        return pick, (high, (spread - high.astype(jnp.float32)).astype(jnp.bfloat16))

    own_pick, own_spread = slots(routes, mixing)
    far_pick, far_spread = slots(
        far_plan[:, :top_count].astype(jnp.int32), far_plan[:, top_count:]
    )

    def after(value, *earlier):
        return lax.optimization_barrier((value, *earlier))[0]

    def whole(value):
        return [exchange(value, "tp", j) for j in range(tp)]

    def picked(pick, values):
        parts = [
            jnp.dot(pick, value, preferred_element_type=jnp.float32)
            .astype(jnp.bfloat16)
            .reshape(half, capacity, width)
            for value in values
        ]
        return jnp.stack(parts, axis=1)

    def send_rows(rows):
        return [exchange(rows[d], "group", 2 * d) for d in range(half)]

    def blend(spread, pieces):
        rows = jnp.concatenate(pieces, axis=0)
        rows_first = (((0,), (0,)), ((), ()))
        return sum(
            lax.dot_general(part, rows, rows_first, preferred_element_type=jnp.float32)
            for part in spread
        )

    def activate(sets):
        rows = sets[0].shape[1]
        (active,) = kernel_call(
            functools.partial(gate_up_kernel, tp),
            [((2 * rows, hidden), jnp.bfloat16)],
            [tp_scalar],
            [gate, up, gain],
            *sets,
            scratch=[
                pltpu.VMEM((tp, rows, width), jnp.float32),
                pltpu.VMEM((2 * rows, tp * width), jnp.bfloat16),
                pltpu.VMEM(gate.shape, jnp.bfloat16),
                pltpu.VMEM(up.shape, jnp.bfloat16),
                pltpu.VMEM(gain.shape, jnp.float32),
                dma((1 + 4 * len(tiles(hidden)),)),
            ],
        )
        return active

    def project_down(actives):
        rows = actives[0].shape[0] // 2
        return kernel_call(
            down_kernel,
            [((rows, width), jnp.bfloat16)] * 2,
            [tp_scalar],
            [down],
            *actives,
            scratch=[
                pltpu.VMEM(down.shape, jnp.bfloat16),
                pltpu.VMEM((2 * rows, width), jnp.float32),
                dma((PARTS * tp,)),
            ],
        )

    def add_halves(mine, theirs):
        summed = mine.astype(jnp.float32) + exchange(theirs, "group", 1).astype(jnp.float32)
        return summed.astype(jnp.bfloat16).reshape(half, capacity, width)

    far_blocks = whole(exchange(state_sent, "group", experts))
    own_pieces = send_rows(picked(own_pick, own_blocks))
    far_sent = picked(far_pick, far_blocks)
    far_pieces = send_rows(far_sent)
    own_rows = jnp.concatenate([after(piece, far_sent) for piece in own_pieces], axis=1)
    own_active = activate([own_rows, exchange(own_rows, "group", 1)])
    own_actives = whole(own_active)
    far_rows = jnp.concatenate([after(piece, own_active) for piece in far_pieces], axis=1)
    far_active = activate([far_rows, exchange(far_rows, "group", 1)])
    far_actives = whole(far_active)
    own_actives[0] = after(own_actives[0], far_active)
    own_out = project_down(own_actives)
    far_actives[0] = after(far_actives[0], own_out[0])
    far_out = add_halves(*project_down(far_actives))
    own_out = add_halves(*own_out)
    far_sum = blend(far_spread, send_rows(far_out)).astype(jnp.bfloat16)
    own_back = send_rows(after(own_out, far_sum))
    far_sum = exchange(far_sum, "group", experts)
    own_back = [after(piece, far_sum) for piece in own_back]
    total = own_state + blend(own_spread, own_back) + far_sum.astype(jnp.float32)
    return total.astype(jnp.bfloat16)


def solution(mesh):
    return jax.shard_map(
        on_device,
        mesh=mesh,
        in_specs=(
            P("group", "tp"),
            P("group", "tp"),
            P("group", "tp"),
            P("group", "tp"),
            P("group", None),
            P("group"),
            P("tp"),
            P("tp", None),
            P("group", "tp"),
            P(),
            P("group", None),
            P("group", None),
            P("group", None, "tp"),
            P("group", None, "tp"),
            P("group", None, "tp"),
        ),
        out_specs=P("group", "tp"),
        check_vma=False,
    )
```

profile of v0, /device:TPU:0, one launch (start us, length us, event | category | flops | bytes accessed | tf_op | source)
XLA Modules:
  0.0 123.2 jit_solution(5771084714671108873)
XLA Ops:
  0.0 7.5 %all-to-all-start = ((bf16[16,8,512]{2,1,0:T(8,128)(2,1)}), bf16[16,8,512]{2,1,0:T(8,128)(2,1)S(1)}, u32[]{:S(2)}, u32[]{:S(2)}) async-start(bf16[16,8,512]{2,1,0:T(8,128)(2,1)} %bitcast.129), calls=%async_computation | async-start | bytes 262144 | tf_op jit(solution)/shard_map/all_to_all | solution.py:267
  9.2 1.3 %reshape.141.gain_ref = f32[1,2880]{1,0:T(1,128)} reshape(f32[2880]{0:T(1024)} %param.24) | data formatting | bytes 23040 | tf_op jit(solution)/shard_map/reshape | solution.py:289
  11.9 3.4 %shard_map.145 = (bf16[1024,128]{1,0:T(8,128)(2,1)S(1)}, f32[1024,128]{1,0:T(8,128)S(1)}) custom-call(f32[16]{0:T(128)S(1)} %copy-done, bf16[64,1024]{1,0:T(8,128)(2,1)} %query_ref.1, bf16[64,512]{1,0:T(8,128)(2,1)} %kv_ref.1, bf16[256,512]{1,0:T(8,128)(2,1)} %local_ref.1, f32[64,128]{1,0:T(8,128)S(1)} %get-tuple-element.86.cos_ref, ...), custom_call_target="tpu_custom_call" | custom-call | tf_op jit(solution)/shard_map/pallas_call | solution.py:293
  16.1 2.9 %shard_map.146 = (bf16[64,1024]{1,0:T(8,128)(2,1)S(1)}, bf16[64,1440]{1,0:T(8,128)(2,1)S(1)}) custom-call(s32[1]{0:T(128)} %bitcast.me_ref, bf16[2,1440,1024]{2,1,0:T(8,128)(2,1)} %bitcast.116, bf16[1024,128]{1,0:T(8,128)(2,1)S(1)} %get-tuple-element.33.rotated_ref, f32[1024,128]{1,0:T(8,128)S(1)} %get-tuple-element.34.state_ref, ...), custom_call_target="tpu_custom_call" | custom-call | tf_op jit(solution)/shard_map/pallas_call | solution.py:226
  19.0 1.6 %collective-permute-start = (bf16[64,1440]{1,0:T(8,128)(2,1)S(1)}, bf16[64,1440]{1,0:T(8,128)(2,1)S(1)}, u32[]{:S(2)}, u32[]{:S(2)}) collective-permute-start(bf16[64,1440]{1,0:T(8,128)(2,1)S(1)} %get-tuple-element.38), channel_id=1, source_target_pairs={{0,1},{1,0},{2,3},{3,2},{4,5},{5,4},{6,7},{7,6},{8,9},{9,8},{10,11... | collective-permute-start | bytes 552968 | tf_op jit(solution)/shard_map/ppermute | solution.py:25
  20.6 2.9 %shard_map.147 = (f32[64,1440]{1,0:T(8,128)S(1)}, bf16[64,1440]{1,0:T(8,128)(2,1)S(1)}) custom-call(s32[1]{0:T(128)} %bitcast.me_ref, bf16[2,1440,1024]{2,1,0:T(8,128)(2,1)} %bitcast.117, bf16[64,1440]{1,0:T(8,128)(2,1)} %residual_ref.1, bf16[64,1024]{1,0:T(8,128)(2,1)S(1)} %get-tuple-element.36.attended_ref), custom_call_target="tpu_custom_call" | custom-call | tf_op jit(solution)/shard_map/pallas_call | solution.py:226
  23.4 2.9 %collective-permute-done = bf16[64,1440]{1,0:T(8,128)(2,1)S(1)} collective-permute-done((bf16[64,1440]{1,0:T(8,128)(2,1)S(1)}, bf16[64,1440]{1,0:T(8,128)(2,1)S(1)}, u32[]{:S(2)}, u32[]{:S(2)}) %collective-permute-start) | collective-permute-done | bytes 184352 | tf_op jit(solution)/shard_map/ppermute | solution.py:25
  26.3 1.6 %collective-permute-start.1 = (bf16[64,1440]{1,0:T(8,128)(2,1)S(1)}, bf16[64,1440]{1,0:T(8,128)(2,1)S(1)}, u32[]{:S(2)}, u32[]{:S(2)}) collective-permute-start(bf16[64,1440]{1,0:T(8,128)(2,1)S(1)} %get-tuple-element.40), channel_id=1, source_target_pairs={{0,1},{1,0},{2,3},{3,2},{4,5},{5,4},{6,7},{7,6},{8,9},{9,8},{10,11... | collective-permute-start | bytes 552968 | tf_op jit(solution)/shard_map/ppermute | solution.py:25
  27.9 2.6 %collective-permute-start.3 = (bf16[64,1440]{1,0:T(8,128)(2,1)S(1)}, bf16[64,1440]{1,0:T(8,128)(2,1)S(1)}, u32[]{:S(2)}, u32[]{:S(2)}) collective-permute-start(bf16[64,1440]{1,0:T(8,128)(2,1)S(1)} %fusion.4), channel_id=1, source_target_pairs={{0,16},{2,18},{4,20},{6,22},{8,24},{10,26},{12,28},{14,30},{16,0},... | collective-permute-start | bytes 552968 | tf_op jit(solution)/shard_map/ppermute | solution.py:25
  30.5 2.3 %collective-permute-done.1 = bf16[64,1440]{1,0:T(8,128)(2,1)S(1)} collective-permute-done((bf16[64,1440]{1,0:T(8,128)(2,1)S(1)}, bf16[64,1440]{1,0:T(8,128)(2,1)S(1)}, u32[]{:S(2)}, u32[]{:S(2)}) %collective-permute-start.1) | collective-permute-done | bytes 184352 | tf_op jit(solution)/shard_map/ppermute | solution.py:25
  32.9 2.3 %collective-permute-start.2 = (f32[64,8]{0,1:T(8,128)S(1)}, f32[64,8]{0,1:T(8,128)S(1)}, u32[]{:S(2)}, u32[]{:S(2)}) collective-permute-start(f32[64,8]{0,1:T(8,128)S(1)} %pad_maximum_fusion.5), channel_id=1, source_target_pairs={{0,16},{2,18},{4,20},{6,22},{8,24},{10,26},{12,28},{14,30},{16,0},... | collective-permute-start | bytes 6152 | tf_op jit(solution)/shard_map/ppermute | solution.py:25
  35.4 4.0 %collective-permute-done.3 = bf16[64,1440]{1,0:T(8,128)(2,1)S(1)} collective-permute-done((bf16[64,1440]{1,0:T(8,128)(2,1)S(1)}, bf16[64,1440]{1,0:T(8,128)(2,1)S(1)}, u32[]{:S(2)}, u32[]{:S(2)}) %collective-permute-start.3) | collective-permute-done | bytes 184352 | tf_op jit(solution)/shard_map/ppermute | solution.py:25
  42.1 1.5 %collective-permute-start.6 = (bf16[2,40,1440]{2,1,0:T(8,128)(2,1)S(1)}, bf16[2,40,1440]{2,1,0:T(8,128)(2,1)S(1)}, u32[]{:S(2)}, u32[]{:S(2)}) collective-permute-start(bf16[2,40,1440]{2,1,0:T(8,128)(2,1)S(1)} %get-tuple-element.68), channel_id=1, source_target_pairs={{0,8},{2,10},{4,12},{6,14},{8,0},{10,2},{12,4},{14,6},{16,24},{18,... | collective-permute-start | bytes 691208 | tf_op jit(solution)/shard_map/ppermute | solution.py:25
  45.6 5.1 %collective-permute-done.7 = bf16[2,40,1440]{2,1,0:T(8,128)(2,1)S(1)} collective-permute-done((bf16[2,40,1440]{2,1,0:T(8,128)(2,1)S(1)}, bf16[2,40,1440]{2,1,0:T(8,128)(2,1)S(1)}, u32[]{:S(2)}, u32[]{:S(2)}) %collective-permute-start.7) | collective-permute-done | bytes 230432 | tf_op jit(solution)/shard_map/ppermute | solution.py:25
  50.7 2.8 %collective-permute-done.6 = bf16[2,40,1440]{2,1,0:T(8,128)(2,1)S(1)} collective-permute-done((bf16[2,40,1440]{2,1,0:T(8,128)(2,1)S(1)}, bf16[2,40,1440]{2,1,0:T(8,128)(2,1)S(1)}, u32[]{:S(2)}, u32[]{:S(2)}) %collective-permute-start.6) | collective-permute-done | bytes 230432 | tf_op jit(solution)/shard_map/ppermute | solution.py:25
  54.0 2.0 %collective-permute-start.11 = (bf16[2,40,1440]{2,1,0:T(8,128)(2,1)S(1)}, bf16[2,40,1440]{2,1,0:T(8,128)(2,1)S(1)}, u32[]{:S(2)}, u32[]{:S(2)}) collective-permute-start(bf16[2,40,1440]{2,1,0:T(8,128)(2,1)S(1)} %get-tuple-element.61), channel_id=1, source_target_pairs={{0,12},{2,14},{4,8},{6,10},{8,4},{10,6},{12,0},{14,2},{16,28},{18,... | collective-permute-start | bytes 691208 | tf_op jit(solution)/shard_map/ppermute | solution.py:25
  57.6 5.9 %shard_map.148.refs_0_ = bf16[320,720]{1,0:T(8,128)(2,1)S(1)} custom-call(s32[1]{0:T(128)} %bitcast.me_ref, bf16[720,2880]{1,0:T(8,128)(2,1)} %bitcast.120, bf16[720,2880]{1,0:T(8,128)(2,1)} %bitcast.122, f32[1,2880]{1,0:T(1,128)} %reshape.141.gain_ref, bf16[2,160,1440]{2,1,0:T(8,128)(2,1)S(1)} %constant_dynamic-update-slice_fusion.refs_0_, ...), custom_call_target="tpu_custom_call" | custom-call | tf_op jit(solution)/shard_map/pallas_call | solution.py:226
  63.7 4.6 %collective-permute-done.10 = bf16[2,40,1440]{2,1,0:T(8,128)(2,1)S(1)} collective-permute-done((bf16[2,40,1440]{2,1,0:T(8,128)(2,1)S(1)}, bf16[2,40,1440]{2,1,0:T(8,128)(2,1)S(1)}, u32[]{:S(2)}, u32[]{:S(2)}) %collective-permute-start.10) | collective-permute-done | bytes 230432 | tf_op jit(solution)/shard_map/ppermute | solution.py:25
  68.8 1.6 %collective-permute-start.13 = (bf16[320,720]{1,0:T(8,128)(2,1)S(1)}, bf16[320,720]{1,0:T(8,128)(2,1)S(1)}, u32[]{:S(2)}, u32[]{:S(2)}) collective-permute-start(bf16[320,720]{1,0:T(8,128)(2,1)S(1)} %shard_map.148.refs_0_), channel_id=1, source_target_pairs={{0,1},{1,0},{2,3},{3,2},{4,5},{5,4},{6,7},{7,6},{8,9},{9,8},{10,11... | collective-permute-start | bytes 1382408 | tf_op jit(solution)/shard_map/ppermute | solution.py:25
  71.3 6.1 %shard_map.149.refs_0_ = bf16[320,720]{1,0:T(8,128)(2,1)S(1)} custom-call(s32[1]{0:T(128)} %bitcast.me_ref, bf16[720,2880]{1,0:T(8,128)(2,1)} %bitcast.121, bf16[720,2880]{1,0:T(8,128)(2,1)} %bitcast.123, f32[1,2880]{1,0:T(1,128)} %reshape.141.gain_ref, bf16[2,160,1440]{2,1,0:T(8,128)(2,1)S(1)} %constant_dynamic-update-slice_fusion.4.refs_0_, ...), custom_call_target="tpu_custom_call" | custom-call | tf_op jit(solution)/shard_map/pallas_call | solution.py:226
  77.4 1.6 %collective-permute-start.15 = (bf16[320,720]{1,0:T(8,128)(2,1)S(1)}, bf16[320,720]{1,0:T(8,128)(2,1)S(1)}, u32[]{:S(2)}, u32[]{:S(2)}) collective-permute-start(bf16[320,720]{1,0:T(8,128)(2,1)S(1)} %shard_map.149.refs_0_), channel_id=1, source_target_pairs={{0,1},{1,0},{2,3},{3,2},{4,5},{5,4},{6,7},{7,6},{8,9},{9,8},{10,11... | collective-permute-start | bytes 1382408 | tf_op jit(solution)/shard_map/ppermute | solution.py:25
  79.0 3.8 %collective-permute-done.13.refs_1_ = bf16[320,720]{1,0:T(8,128)(2,1)S(1)} collective-permute-done((bf16[320,720]{1,0:T(8,128)(2,1)S(1)}, bf16[320,720]{1,0:T(8,128)(2,1)S(1)}, u32[]{:S(2)}, u32[]{:S(2)}) %collective-permute-start.13) | collective-permute-done | bytes 460832 | tf_op jit(solution)/shard_map/ppermute | solution.py:25
  82.8 3.5 %shard_map.150 = (bf16[160,1440]{1,0:T(8,128)(2,1)S(1)}, bf16[160,1440]{1,0:T(8,128)(2,1)S(1)}) custom-call(s32[1]{0:T(128)} %bitcast.me_ref, bf16[2,720,1440]{2,1,0:T(8,128)(2,1)} %bitcast.118, bf16[320,720]{1,0:T(8,128)(2,1)S(1)} %shard_map.148.refs_0_, bf16[320,720]{1,0:T(8,128)(2,1)S(1)} %collective-permute-done.13.refs_1_), custom_call_target="tpu_custom_call" | custom-call | tf_op jit(solution)/shard_map/pallas_call | solution.py:226
  86.3 6.6 %collective-permute-done.15.refs_1_ = bf16[320,720]{1,0:T(8,128)(2,1)S(1)} collective-permute-done((bf16[320,720]{1,0:T(8,128)(2,1)S(1)}, bf16[320,720]{1,0:T(8,128)(2,1)S(1)}, u32[]{:S(2)}, u32[]{:S(2)}) %collective-permute-start.15) | collective-permute-done | bytes 460832 | tf_op jit(solution)/shard_map/ppermute | solution.py:25
  92.9 3.5 %shard_map.151 = (bf16[160,1440]{1,0:T(8,128)(2,1)S(1)}, bf16[160,1440]{1,0:T(8,128)(2,1)S(1)}) custom-call(s32[1]{0:T(128)} %bitcast.me_ref, bf16[2,720,1440]{2,1,0:T(8,128)(2,1)} %bitcast.119, bf16[320,720]{1,0:T(8,128)(2,1)S(1)} %shard_map.149.refs_0_, bf16[320,720]{1,0:T(8,128)(2,1)S(1)} %collective-permute-done.15.refs_1_), custom_call_target="tpu_custom_call" | custom-call | tf_op jit(solution)/shard_map/pallas_call | solution.py:226
  99.8 1.3 %collective-permute-start.18 = (bf16[40,1440]{1,0:T(8,128)(2,1)S(1)}, bf16[40,1440]{1,0:T(8,128)(2,1)S(1)}, u32[]{:S(2)}, u32[]{:S(2)}) collective-permute-start(bf16[40,1440]{1,0:T(8,128)(2,1)S(1)} %get-tuple-element.75), channel_id=1, source_target_pairs={{0,8},{2,10},{4,12},{6,14},{8,0},{10,2},{12,4},{14,6},{16,24},{18,... | collective-permute-start | bytes 345608 | tf_op jit(solution)/shard_map/ppermute | solution.py:25
  102.2 1.8 %collective-permute-done.17 = bf16[40,1440]{1,0:T(8,128)(2,1)S(1)} collective-permute-done((bf16[40,1440]{1,0:T(8,128)(2,1)S(1)}, bf16[40,1440]{1,0:T(8,128)(2,1)S(1)}, u32[]{:S(2)}, u32[]{:S(2)}) %collective-permute-start.17) | collective-permute-done | bytes 115232 | tf_op jit(solution)/shard_map/ppermute | solution.py:25
  104.0 2.0 %collective-permute-done.18 = bf16[40,1440]{1,0:T(8,128)(2,1)S(1)} collective-permute-done((bf16[40,1440]{1,0:T(8,128)(2,1)S(1)}, bf16[40,1440]{1,0:T(8,128)(2,1)S(1)}, u32[]{:S(2)}, u32[]{:S(2)}) %collective-permute-start.18) | collective-permute-done | bytes 115232 | tf_op jit(solution)/shard_map/ppermute | solution.py:25
  106.0 1.8 %collective-permute-done.19 = bf16[40,1440]{1,0:T(8,128)(2,1)S(1)} collective-permute-done((bf16[40,1440]{1,0:T(8,128)(2,1)S(1)}, bf16[40,1440]{1,0:T(8,128)(2,1)S(1)}, u32[]{:S(2)}, u32[]{:S(2)}) %collective-permute-start.19) | collective-permute-done | bytes 115232 | tf_op jit(solution)/shard_map/ppermute | solution.py:25
  108.3 2.9 %collective-permute-start.20 = (bf16[64,1440]{1,0:T(8,128)(2,1)S(1)}, bf16[64,1440]{1,0:T(8,128)(2,1)S(1)}, u32[]{:S(2)}, u32[]{:S(2)}) collective-permute-start(bf16[64,1440]{1,0:T(8,128)(2,1)S(1)} %fusion.2), channel_id=1, source_target_pairs={{0,16},{2,18},{4,20},{6,22},{8,24},{10,26},{12,28},{14,30},{16,0},... | collective-permute-start | bytes 552968 | tf_op jit(solution)/shard_map/ppermute | solution.py:25
  111.2 2.7 %collective-permute-start.23 = (bf16[40,1440]{1,0:T(8,128)(2,1)S(1)}, bf16[40,1440]{1,0:T(8,128)(2,1)S(1)}, u32[]{:S(2)}, u32[]{:S(2)}) collective-permute-start(bf16[40,1440]{1,0:T(8,128)(2,1)S(1)} %get-tuple-element.69), channel_id=1, source_target_pairs={{0,12},{2,14},{4,8},{6,10},{8,4},{10,6},{12,0},{14,2},{16,28},{18,... | collective-permute-start | bytes 345608 | tf_op jit(solution)/shard_map/ppermute | solution.py:25
  114.8 6.1 %collective-permute-done.23 = bf16[40,1440]{1,0:T(8,128)(2,1)S(1)} collective-permute-done((bf16[40,1440]{1,0:T(8,128)(2,1)S(1)}, bf16[40,1440]{1,0:T(8,128)(2,1)S(1)}, u32[]{:S(2)}, u32[]{:S(2)}) %collective-permute-start.23) | collective-permute-done | bytes 115232 | tf_op jit(solution)/shard_map/ppermute | solution.py:25
  (81 shorter events, 19.9 us)
Async XLA Ops:
  0.0 20.6 %copy-start.1 = (f32[64,4]{0,1:T(4,128)S(1)}, f32[64,4]{0,1:T(4,128)}, u32[]{:S(2)}) copy-start(f32[64,4]{0,1:T(4,128)} %param.26) | copy-start | bytes 3076
  0.0 16.1 %all-to-all-start = ((bf16[16,8,512]{2,1,0:T(8,128)(2,1)}), bf16[16,8,512]{2,1,0:T(8,128)(2,1)S(1)}, u32[]{:S(2)}, u32[]{:S(2)}) async-start(bf16[16,8,512]{2,1,0:T(8,128)(2,1)} %bitcast.129), calls=%async_computation | async-start | bytes 262144 | tf_op jit(solution)/shard_map/all_to_all | solution.py:267
  11.3 0.7 copy-start
  19.0 7.3 %collective-permute-start = (bf16[64,1440]{1,0:T(8,128)(2,1)S(1)}, bf16[64,1440]{1,0:T(8,128)(2,1)S(1)}, u32[]{:S(2)}, u32[]{:S(2)}) collective-permute-start(bf16[64,1440]{1,0:T(8,128)(2,1)S(1)} %get-tuple-element.38), channel_id=1, source_target_pairs={{0,1},{1,0},{2,3},{3,2},{4,5},{5,4},{6,7},{7,6},{8,9},{9,8},{10,11... | collective-permute-start | bytes 552968 | tf_op jit(solution)/shard_map/ppermute | solution.py:25
  26.3 6.5 %collective-permute-start.1 = (bf16[64,1440]{1,0:T(8,128)(2,1)S(1)}, bf16[64,1440]{1,0:T(8,128)(2,1)S(1)}, u32[]{:S(2)}, u32[]{:S(2)}) collective-permute-start(bf16[64,1440]{1,0:T(8,128)(2,1)S(1)} %get-tuple-element.40), channel_id=1, source_target_pairs={{0,1},{1,0},{2,3},{3,2},{4,5},{5,4},{6,7},{7,6},{8,9},{9,8},{10,11... | collective-permute-start | bytes 552968 | tf_op jit(solution)/shard_map/ppermute | solution.py:25
  27.9 11.5 %collective-permute-start.3 = (bf16[64,1440]{1,0:T(8,128)(2,1)S(1)}, bf16[64,1440]{1,0:T(8,128)(2,1)S(1)}, u32[]{:S(2)}, u32[]{:S(2)}) collective-permute-start(bf16[64,1440]{1,0:T(8,128)(2,1)S(1)} %fusion.4), channel_id=1, source_target_pairs={{0,16},{2,18},{4,20},{6,22},{8,24},{10,26},{12,28},{14,30},{16,0},... | collective-permute-start | bytes 552968 | tf_op jit(solution)/shard_map/ppermute | solution.py:25
  32.9 7.0 %collective-permute-start.2 = (f32[64,8]{0,1:T(8,128)S(1)}, f32[64,8]{0,1:T(8,128)S(1)}, u32[]{:S(2)}, u32[]{:S(2)}) collective-permute-start(f32[64,8]{0,1:T(8,128)S(1)} %pad_maximum_fusion.5), channel_id=1, source_target_pairs={{0,16},{2,18},{4,20},{6,22},{8,24},{10,26},{12,28},{14,30},{16,0},... | collective-permute-start | bytes 6152 | tf_op jit(solution)/shard_map/ppermute | solution.py:25
  39.4 6.0 %collective-permute-start.4 = (bf16[64,1440]{1,0:T(8,128)(2,1)S(1)}, bf16[64,1440]{1,0:T(8,128)(2,1)S(1)}, u32[]{:S(2)}, u32[]{:S(2)}) collective-permute-start(bf16[64,1440]{1,0:T(8,128)(2,1)S(1)} %collective-permute-done.3), channel_id=1, source_target_pairs={{0,1},{1,0},{2,3},{3,2},{4,5},{5,4},{6,7},{7,6},{8,9},{9,8},{10,11... | collective-permute-start | bytes 552968 | tf_op jit(solution)/shard_map/ppermute | solution.py:25
  40.8 9.9 %collective-permute-start.7 = (bf16[2,40,1440]{2,1,0:T(8,128)(2,1)S(1)}, bf16[2,40,1440]{2,1,0:T(8,128)(2,1)S(1)}, u32[]{:S(2)}, u32[]{:S(2)}) collective-permute-start(bf16[2,40,1440]{2,1,0:T(8,128)(2,1)S(1)} %get-tuple-element.65), channel_id=1, source_target_pairs={{0,12},{2,14},{4,8},{6,10},{8,4},{10,6},{12,0},{14,2},{16,28},{18,... | collective-permute-start | bytes 691208 | tf_op jit(solution)/shard_map/ppermute | solution.py:25
  42.1 11.4 %collective-permute-start.6 = (bf16[2,40,1440]{2,1,0:T(8,128)(2,1)S(1)}, bf16[2,40,1440]{2,1,0:T(8,128)(2,1)S(1)}, u32[]{:S(2)}, u32[]{:S(2)}) collective-permute-start(bf16[2,40,1440]{2,1,0:T(8,128)(2,1)S(1)} %get-tuple-element.68), channel_id=1, source_target_pairs={{0,8},{2,10},{4,12},{6,14},{8,0},{10,2},{12,4},{14,6},{16,24},{18,... | collective-permute-start | bytes 691208 | tf_op jit(solution)/shard_map/ppermute | solution.py:25
  43.7 10.1 %collective-permute-start.5 = (bf16[2,40,1440]{2,1,0:T(8,128)(2,1)S(1)}, bf16[2,40,1440]{2,1,0:T(8,128)(2,1)S(1)}, u32[]{:S(2)}, u32[]{:S(2)}) collective-permute-start(bf16[2,40,1440]{2,1,0:T(8,128)(2,1)S(1)} %get-tuple-element.67), channel_id=1, source_target_pairs={{0,4},{2,6},{4,0},{6,2},{8,12},{10,14},{12,8},{14,10},{16,20},{18,... | collective-permute-start | bytes 691208 | tf_op jit(solution)/shard_map/ppermute | solution.py:25
  53.8 3.7 %collective-permute-start.8 = (bf16[2,160,1440]{2,1,0:T(8,128)(2,1)S(1)}, bf16[2,160,1440]{2,1,0:T(8,128)(2,1)S(1)}, u32[]{:S(2)}, u32[]{:S(2)}) collective-permute-start(bf16[2,160,1440]{2,1,0:T(8,128)(2,1)S(1)} %constant_dynamic-update-slice_fusion.refs_0_), channel_id=1, source_target_pairs={{0,2},{2,0},{4,6},{6,4},{8,10},{10,8},{12,14},{14,12},{16,18},{18,... | collective-permute-start | bytes 2764808 | tf_op jit(solution)/shard_map/ppermute | solution.py:25
  54.0 9.8 %collective-permute-start.11 = (bf16[2,40,1440]{2,1,0:T(8,128)(2,1)S(1)}, bf16[2,40,1440]{2,1,0:T(8,128)(2,1)S(1)}, u32[]{:S(2)}, u32[]{:S(2)}) collective-permute-start(bf16[2,40,1440]{2,1,0:T(8,128)(2,1)S(1)} %get-tuple-element.61), channel_id=1, source_target_pairs={{0,12},{2,14},{4,8},{6,10},{8,4},{10,6},{12,0},{14,2},{16,28},{18,... | collective-permute-start | bytes 691208 | tf_op jit(solution)/shard_map/ppermute | solution.py:25
  56.0 12.3 %collective-permute-start.10 = (bf16[2,40,1440]{2,1,0:T(8,128)(2,1)S(1)}, bf16[2,40,1440]{2,1,0:T(8,128)(2,1)S(1)}, u32[]{:S(2)}, u32[]{:S(2)}) collective-permute-start(bf16[2,40,1440]{2,1,0:T(8,128)(2,1)S(1)} %get-tuple-element.64), channel_id=1, source_target_pairs={{0,8},{2,10},{4,12},{6,14},{8,0},{10,2},{12,4},{14,6},{16,24},{18,... | collective-permute-start | bytes 691208 | tf_op jit(solution)/shard_map/ppermute | solution.py:25
  56.7 11.9 %collective-permute-start.9 = (bf16[2,40,1440]{2,1,0:T(8,128)(2,1)S(1)}, bf16[2,40,1440]{2,1,0:T(8,128)(2,1)S(1)}, u32[]{:S(2)}, u32[]{:S(2)}) collective-permute-start(bf16[2,40,1440]{2,1,0:T(8,128)(2,1)S(1)} %get-tuple-element.63), channel_id=1, source_target_pairs={{0,4},{2,6},{4,0},{6,2},{8,12},{10,14},{12,8},{14,10},{16,20},{18,... | collective-permute-start | bytes 691208 | tf_op jit(solution)/shard_map/ppermute | solution.py:25
  68.7 2.6 %collective-permute-start.12 = (bf16[2,160,1440]{2,1,0:T(8,128)(2,1)S(1)}, bf16[2,160,1440]{2,1,0:T(8,128)(2,1)S(1)}, u32[]{:S(2)}, u32[]{:S(2)}) collective-permute-start(bf16[2,160,1440]{2,1,0:T(8,128)(2,1)S(1)} %constant_dynamic-update-slice_fusion.4.refs_0_), channel_id=1, source_target_pairs={{0,2},{2,0},{4,6},{6,4},{8,10},{10,8},{12,14},{14,12},{16,18},{18,... | collective-permute-start | bytes 2764808 | tf_op jit(solution)/shard_map/ppermute | solution.py:25
  68.8 14.1 %collective-permute-start.13 = (bf16[320,720]{1,0:T(8,128)(2,1)S(1)}, bf16[320,720]{1,0:T(8,128)(2,1)S(1)}, u32[]{:S(2)}, u32[]{:S(2)}) collective-permute-start(bf16[320,720]{1,0:T(8,128)(2,1)S(1)} %shard_map.148.refs_0_), channel_id=1, source_target_pairs={{0,1},{1,0},{2,3},{3,2},{4,5},{5,4},{6,7},{7,6},{8,9},{9,8},{10,11... | collective-permute-start | bytes 1382408 | tf_op jit(solution)/shard_map/ppermute | solution.py:25
  77.4 15.5 %collective-permute-start.15 = (bf16[320,720]{1,0:T(8,128)(2,1)S(1)}, bf16[320,720]{1,0:T(8,128)(2,1)S(1)}, u32[]{:S(2)}, u32[]{:S(2)}) collective-permute-start(bf16[320,720]{1,0:T(8,128)(2,1)S(1)} %shard_map.149.refs_0_), channel_id=1, source_target_pairs={{0,1},{1,0},{2,3},{3,2},{4,5},{5,4},{6,7},{7,6},{8,9},{9,8},{10,11... | collective-permute-start | bytes 1382408 | tf_op jit(solution)/shard_map/ppermute | solution.py:25
  96.4 1.9 %collective-permute-start.16 = (bf16[160,1440]{1,0:T(8,128)(2,1)S(1)}, bf16[160,1440]{1,0:T(8,128)(2,1)S(1)}, u32[]{:S(2)}, u32[]{:S(2)}) collective-permute-start(bf16[160,1440]{1,0:T(8,128)(2,1)S(1)} %get-tuple-element.55), channel_id=1, source_target_pairs={{0,2},{2,0},{4,6},{6,4},{8,10},{10,8},{12,14},{14,12},{16,18},{18,... | collective-permute-start | bytes 1382408 | tf_op jit(solution)/shard_map/ppermute | solution.py:25
  96.8 5.3 %collective-permute-start.14 = (bf16[160,1440]{1,0:T(8,128)(2,1)S(1)}, bf16[160,1440]{1,0:T(8,128)(2,1)S(1)}, u32[]{:S(2)}, u32[]{:S(2)}) collective-permute-start(bf16[160,1440]{1,0:T(8,128)(2,1)S(1)} %get-tuple-element.52), channel_id=1, source_target_pairs={{0,2},{2,0},{4,6},{6,4},{8,10},{10,8},{12,14},{14,12},{16,18},{18,... | collective-permute-start | bytes 1382408 | tf_op jit(solution)/shard_map/ppermute | solution.py:25
  98.5 5.4 %collective-permute-start.17 = (bf16[40,1440]{1,0:T(8,128)(2,1)S(1)}, bf16[40,1440]{1,0:T(8,128)(2,1)S(1)}, u32[]{:S(2)}, u32[]{:S(2)}) collective-permute-start(bf16[40,1440]{1,0:T(8,128)(2,1)S(1)} %get-tuple-element.76), channel_id=1, source_target_pairs={{0,4},{2,6},{4,0},{6,2},{8,12},{10,14},{12,8},{14,10},{16,20},{18,... | collective-permute-start | bytes 345608 | tf_op jit(solution)/shard_map/ppermute | solution.py:25
  99.8 6.2 %collective-permute-start.18 = (bf16[40,1440]{1,0:T(8,128)(2,1)S(1)}, bf16[40,1440]{1,0:T(8,128)(2,1)S(1)}, u32[]{:S(2)}, u32[]{:S(2)}) collective-permute-start(bf16[40,1440]{1,0:T(8,128)(2,1)S(1)} %get-tuple-element.75), channel_id=1, source_target_pairs={{0,8},{2,10},{4,12},{6,14},{8,0},{10,2},{12,4},{14,6},{16,24},{18,... | collective-permute-start | bytes 345608 | tf_op jit(solution)/shard_map/ppermute | solution.py:25
  101.1 6.7 %collective-permute-start.19 = (bf16[40,1440]{1,0:T(8,128)(2,1)S(1)}, bf16[40,1440]{1,0:T(8,128)(2,1)S(1)}, u32[]{:S(2)}, u32[]{:S(2)}) collective-permute-start(bf16[40,1440]{1,0:T(8,128)(2,1)S(1)} %get-tuple-element.74), channel_id=1, source_target_pairs={{0,12},{2,14},{4,8},{6,10},{8,4},{10,6},{12,0},{14,2},{16,28},{18,... | collective-permute-start | bytes 345608 | tf_op jit(solution)/shard_map/ppermute | solution.py:25
  108.3 12.6 %collective-permute-start.20 = (bf16[64,1440]{1,0:T(8,128)(2,1)S(1)}, bf16[64,1440]{1,0:T(8,128)(2,1)S(1)}, u32[]{:S(2)}, u32[]{:S(2)}) collective-permute-start(bf16[64,1440]{1,0:T(8,128)(2,1)S(1)} %fusion.2), channel_id=1, source_target_pairs={{0,16},{2,18},{4,20},{6,22},{8,24},{10,26},{12,28},{14,30},{16,0},... | collective-permute-start | bytes 552968 | tf_op jit(solution)/shard_map/ppermute | solution.py:25
  111.2 9.6 %collective-permute-start.23 = (bf16[40,1440]{1,0:T(8,128)(2,1)S(1)}, bf16[40,1440]{1,0:T(8,128)(2,1)S(1)}, u32[]{:S(2)}, u32[]{:S(2)}) collective-permute-start(bf16[40,1440]{1,0:T(8,128)(2,1)S(1)} %get-tuple-element.69), channel_id=1, source_target_pairs={{0,12},{2,14},{4,8},{6,10},{8,4},{10,6},{12,0},{14,2},{16,28},{18,... | collective-permute-start | bytes 345608 | tf_op jit(solution)/shard_map/ppermute | solution.py:25
  113.9 8.1 %collective-permute-start.22 = (bf16[40,1440]{1,0:T(8,128)(2,1)S(1)}, bf16[40,1440]{1,0:T(8,128)(2,1)S(1)}, u32[]{:S(2)}, u32[]{:S(2)}) collective-permute-start(bf16[40,1440]{1,0:T(8,128)(2,1)S(1)} %get-tuple-element.70), channel_id=1, source_target_pairs={{0,8},{2,10},{4,12},{6,14},{8,0},{10,2},{12,4},{14,6},{16,24},{18,... | collective-permute-start | bytes 345608 | tf_op jit(solution)/shard_map/ppermute | solution.py:25
  114.2 7.8 %collective-permute-start.21 = (bf16[40,1440]{1,0:T(8,128)(2,1)S(1)}, bf16[40,1440]{1,0:T(8,128)(2,1)S(1)}, u32[]{:S(2)}, u32[]{:S(2)}) collective-permute-start(bf16[40,1440]{1,0:T(8,128)(2,1)S(1)} %get-tuple-element.71), channel_id=1, source_target_pairs={{0,4},{2,6},{4,0},{6,2},{8,12},{10,14},{12,8},{14,10},{16,20},{18,... | collective-permute-start | bytes 345608 | tf_op jit(solution)/shard_map/ppermute | solution.py:25
where the time goes:
time: 124 us; the launch traced here: 123 us
  waiting for transfers between devices  48.1 us (39%)
  starting transfers between devices  37.2 us (30%)
  Pallas kernels  28.2 us (23%)
  other arithmetic  3.31 us (3%)
  matrix products  2.97 us (2%)
  local copies, waits for them, and re-layouts  2.41 us (2%)
    ppermute x24, waiting for transfers between devices, exchange(): return lax.ppermute(value, axis, [(i, i ^ offset) for i in range(size)])  48.1 us
    ppermute x24, starting transfers between devices, exchange(): return lax.ppermute(value, axis, [(i, i ^ offset) for i in range(size)])  29.7 us
    pallas_call x6, Pallas kernels, kernel_call(): pl.pallas_call(kernel, out_shape=[pltpu.VMEM(shape, dtype) for shape, dty...  24.8 us
    all_to_all x1, starting transfers between devices, on_device(): lax.all_to_all(remote_pool.reshape(groups, -1, lane_count), 'group', spli...  7.52 us
    pallas_call x1, Pallas kernels, on_device(): pl.pallas_call(local_kernel, out_shape=[pltpu.VMEM((states, 2 * HEAD), jn...  3.41 us
  transfers between devices with their start and end apart: 25, of which 19 were waited for; matrix products, arithmetic and copies ran while one was open for 5% of the time, Pallas kernels for 18%

commit v1 on v0

--- a/solution.py
+++ b/solution.py
@@ -151,16 +151,12 @@
         ref[...] = dot_nt(attended, held_ref[j]).astype(jnp.bfloat16)
 
 
-def own_columns_kernel(
-    me_ref, weight_ref, residual_ref, attended_ref, out_ref, sent_ref, held_ref, rows_ref, sems
-):
+def own_columns_kernel(me_ref, weight_ref, residual_ref, attended_ref, out_ref, held_ref, rows_ref, sems):
     copies = split_copies(weight_ref.at[me_ref[0]], held_ref, sems, 0, PARTS)
     copies.append(pltpu.make_async_copy(residual_ref, rows_ref, sems.at[PARTS]))
     start_all(copies)
     wait_all(copies)
-    terms = rows_ref[...].astype(jnp.float32) + dot_nt(attended_ref[...], held_ref[...])
-    out_ref[...] = terms
-    sent_ref[...] = terms.astype(jnp.bfloat16)
+    out_ref[...] = rows_ref[...].astype(jnp.float32) + dot_nt(attended_ref[...], held_ref[...])
 
 
 def tiles(size):
@@ -169,7 +165,9 @@
 
 def gate_up_kernel(parts, me_ref, gate_ref, up_ref, gain_ref, *refs):
     sets, (out_ref, place_ref, row_ref, gate_held, up_held, gain_held, sems) = refs[:-7], refs[-7:]
-    rows, width = sets[0].shape[1:]
+    rows = sets[0].shape[-2]
+    if len(sets[0].shape) == 2:
+        sets = [sets[s : s + parts] for s in range(0, len(sets), parts)]
     features, hidden = gate_ref.shape[1], gate_ref.shape[0]
     gain_copy = pltpu.make_async_copy(gain_ref, gain_held, sems.at[0])
     gain_copy.start()
@@ -182,7 +180,7 @@
     me = me_ref[0]
     gain_copy.wait()
     for s, ref in enumerate(sets):
-        held = [ref[j].astype(jnp.float32) for j in range(parts)]
+        held = [(ref[j][...] if isinstance(ref, tuple) else ref[j]).astype(jnp.float32) for j in range(parts)]
         square = sum(jnp.sum(h * h, axis=1, keepdims=True) for h in held)
         scale = lax.rsqrt(square / features + EPSILON)
         for j in range(parts):
@@ -316,9 +314,9 @@
         scratch=[pltpu.VMEM((tp - 1, *weight.shape[1:]), jnp.bfloat16), dma((PARTS * (tp - 1),))],
     )
     arriving = [exchange(other, "tp", j + 1) for j, other in enumerate(others)]
-    own_state, own_terms = kernel_call(
+    (own_state,) = kernel_call(
         own_columns_kernel,
-        [(residual.shape, jnp.float32), (residual.shape, jnp.bfloat16)],
+        [(residual.shape, jnp.float32)],
         [tp_scalar],
         [weight, residual],
         lax.optimization_barrier((attended, gain))[0],
@@ -331,19 +329,13 @@
     for term in arriving:
         own_state = own_state + term.astype(jnp.float32)
     state_sent = own_state.astype(jnp.bfloat16)
-    if tp == 2:
-        own_terms = lax.optimization_barrier((own_terms, state_sent))[0]
-        other_state = exchange(own_terms, "tp", 1).astype(jnp.float32) + others[0].astype(jnp.float32)
-        own_blocks = [state_sent, other_state.astype(jnp.bfloat16)]
-    else:
-        own_blocks = [exchange(state_sent, "tp", j) for j in range(tp)]
 
     top_count = routes.shape[1]
     capacity = 5 * block_len * top_count // (4 * experts)
     half = experts // 2
     mixing = route_weights / jnp.sum(route_weights, axis=1, keepdims=True)
     plan = jnp.concatenate([routes.astype(jnp.float32), mixing], axis=1)
-    far_plan = exchange(lax.optimization_barrier((plan, own_blocks[-1]))[0], "group", experts)
+    far_plan = exchange(lax.optimization_barrier((plan, state_sent))[0], "group", experts)
 
     def slots(chosen_experts, weights):
         chosen = (chosen_experts ^ me_expert)[:, :, None] == jnp.arange(half, dtype=jnp.int32)
@@ -362,9 +354,6 @@
         return pick, (high, (spread - high.astype(jnp.float32)).astype(jnp.bfloat16))
 
     own_pick, own_spread = slots(routes, mixing)
-    far_pick, far_spread = slots(
-        far_plan[:, :top_count].astype(jnp.int32), far_plan[:, top_count:]
-    )
 
     def after(value, *earlier):
         return lax.optimization_barrier((value, *earlier))[0]
@@ -393,7 +382,7 @@
         )
 
     def activate(sets):
-        rows = sets[0].shape[1]
+        rows = sets[0].shape[-2]
         (active,) = kernel_call(
             functools.partial(gate_up_kernel, tp),
             [((2 * rows, hidden), jnp.bfloat16)],
@@ -430,12 +419,18 @@
         summed = mine.astype(jnp.float32) + exchange(theirs, "group", 1).astype(jnp.float32)
         return summed.astype(jnp.bfloat16).reshape(half, capacity, width)
 
-    far_blocks = whole(exchange(state_sent, "group", experts))
-    own_pieces = send_rows(picked(own_pick, own_blocks))
-    far_sent = picked(far_pick, far_blocks)
+    far_state = exchange(state_sent, "group", experts)
+    own_pieces = send_rows(picked(own_pick, [state_sent]))
+    own_rows = jnp.concatenate([after(piece[0], far_state) for piece in own_pieces], axis=0)
+    far_plan = after(far_plan, own_rows)
+    far_pick, far_spread = slots(
+        far_plan[:, :top_count].astype(jnp.int32), far_plan[:, top_count:]
+    )
+    own_rows = whole(own_rows)
+    far_sent = picked(far_pick, whole(far_state))
     far_pieces = send_rows(far_sent)
-    own_rows = jnp.concatenate([after(piece, far_sent) for piece in own_pieces], axis=1)
-    own_active = activate([own_rows, exchange(own_rows, "group", 1)])
+    own_pairs = [own_rows[0], *[after(rows, far_pieces[1]) for rows in own_rows[1:]]]
+    own_active = activate([*own_rows, *[exchange(rows, "group", 1) for rows in own_pairs]])
     own_actives = whole(own_active)
     far_rows = jnp.concatenate([after(piece, own_active) for piece in far_pieces], axis=1)
     far_active = activate([far_rows, exchange(far_rows, "group", 1)])
@@ -446,10 +441,8 @@
     far_out = add_halves(*project_down(far_actives))
     own_out = add_halves(*own_out)
     far_sum = blend(far_spread, send_rows(far_out)).astype(jnp.bfloat16)
-    own_back = send_rows(after(own_out, far_sum))
     far_sum = exchange(far_sum, "group", experts)
-    own_back = [after(piece, far_sum) for piece in own_back]
-    total = own_state + blend(own_spread, own_back) + far_sum.astype(jnp.float32)
+    total = own_state + blend(own_spread, send_rows(own_out)) + far_sum.astype(jnp.float32)
     return total.astype(jnp.bfloat16)
 
 

time: 124 us -> 129 us (1.040)
  waiting for transfers between devices: 48.1 us -> 58.9 us
  starting transfers between devices: 37.2 us -> 32 us
    ppermute x24 -> x25, waiting for transfers between devices: 48.1 us -> 58.9 us  [exchange(): return lax.ppermute(value, axis, [(i, i ^ offset) for i in range(size)])]
    ppermute x24 -> x25, starting transfers between devices: 29.7 us -> 24.6 us  [exchange(): return lax.ppermute(value, axis, [(i, i ^ offset) for i in range(size)])]
  transfers between devices with their start and end apart: 25 -> 26, of which waited for: 19 -> 17; matrix products, arithmetic and copies ran while one was open for 5% -> 5% of each run, Pallas kernels for 18% -> 20%
where the time goes in v1:
time: 129 us
  waiting for transfers between devices  58.9 us (46%)
  starting transfers between devices  32 us (25%)
  Pallas kernels  28.3 us (22%)
  other arithmetic  3.26 us (3%)
  matrix products  2.7 us (2%)
  local copies, waits for them, and re-layouts  2.37 us (2%)
    ppermute x25, waiting for transfers between devices, exchange(): return lax.ppermute(value, axis, [(i, i ^ offset) for i in range(size)])  58.9 us
    pallas_call x6, Pallas kernels, kernel_call(): pl.pallas_call(kernel, out_shape=[pltpu.VMEM(shape, dtype) for shape, dty...  24.8 us
    ppermute x25, starting transfers between devices, exchange(): return lax.ppermute(value, axis, [(i, i ^ offset) for i in range(size)])  24.6 us
    all_to_all x1, starting transfers between devices, on_device(): lax.all_to_all(remote_pool.reshape(groups, -1, lane_count), 'group', spli...  7.39 us
    pallas_call x1, Pallas kernels, on_device(): pl.pallas_call(local_kernel, out_shape=[pltpu.VMEM((states, 2 * HEAD), jn...  3.41 us
  transfers between devices with their start and end apart: 26, of which 17 were waited for; matrix products, arithmetic and copies ran while one was open for 5% of the time, Pallas kernels for 20%

profile of v1, /device:TPU:0, one launch (start us, length us, event | category | flops | bytes accessed | tf_op | source)
XLA Modules:
  0.0 128.5 jit_solution(17443876295191297767)
XLA Ops:
  0.0 7.4 %all-to-all-start = ((bf16[16,8,512]{2,1,0:T(8,128)(2,1)}), bf16[16,8,512]{2,1,0:T(8,128)(2,1)S(1)}, u32[]{:S(2)}, u32[]{:S(2)}) async-start(bf16[16,8,512]{2,1,0:T(8,128)(2,1)} %bitcast.112), calls=%async_computation | async-start | bytes 262144 | tf_op jit(solution)/shard_map/all_to_all | solution.py:265
  11.9 3.4 %shard_map.145 = (bf16[1024,128]{1,0:T(8,128)(2,1)S(1)}, f32[1024,128]{1,0:T(8,128)S(1)}) custom-call(f32[16]{0:T(128)S(1)} %copy-done, bf16[64,1024]{1,0:T(8,128)(2,1)} %query_ref.1, bf16[64,512]{1,0:T(8,128)(2,1)} %kv_ref.1, bf16[256,512]{1,0:T(8,128)(2,1)} %local_ref.1, f32[64,128]{1,0:T(8,128)S(1)} %get-tuple-element.72.cos_ref, ...), custom_call_target="tpu_custom_call" | custom-call | tf_op jit(solution)/shard_map/pallas_call | solution.py:291
  16.1 2.9 %shard_map.146 = (bf16[64,1024]{1,0:T(8,128)(2,1)S(1)}, bf16[64,1440]{1,0:T(8,128)(2,1)S(1)}) custom-call(s32[1]{0:T(128)} %bitcast.me_ref, bf16[2,1440,1024]{2,1,0:T(8,128)(2,1)} %bitcast.102, bf16[1024,128]{1,0:T(8,128)(2,1)S(1)} %get-tuple-element.27.rotated_ref, f32[1024,128]{1,0:T(8,128)S(1)} %get-tuple-element.28.state_ref, ...), custom_call_target="tpu_custom_call" | custom-call | tf_op jit(solution)/shard_map/pallas_call | solution.py:224
  19.0 1.6 %collective-permute-start = (bf16[64,1440]{1,0:T(8,128)(2,1)S(1)}, bf16[64,1440]{1,0:T(8,128)(2,1)S(1)}, u32[]{:S(2)}, u32[]{:S(2)}) collective-permute-start(bf16[64,1440]{1,0:T(8,128)(2,1)S(1)} %get-tuple-element.31), channel_id=1, source_target_pairs={{0,1},{1,0},{2,3},{3,2},{4,5},{5,4},{6,7},{7,6},{8,9},{9,8},{10,11... | collective-permute-start | bytes 552968 | tf_op jit(solution)/shard_map/ppermute | solution.py:25
  20.8 2.9 %shard_map.147 = f32[64,1440]{1,0:T(8,128)S(1)} custom-call(s32[1]{0:T(128)} %bitcast.me_ref, bf16[2,1440,1024]{2,1,0:T(8,128)(2,1)} %bitcast.103, bf16[64,1440]{1,0:T(8,128)(2,1)} %residual_ref.1, bf16[64,1024]{1,0:T(8,128)(2,1)S(1)} %get-tuple-element.30.attended_ref), custom_call_target="tpu_custom_call" | custom-call | tf_op jit(solution)/shard_map/pallas_call | solution.py:224
  23.7 2.5 %collective-permute-done = bf16[64,1440]{1,0:T(8,128)(2,1)S(1)} collective-permute-done((bf16[64,1440]{1,0:T(8,128)(2,1)S(1)}, bf16[64,1440]{1,0:T(8,128)(2,1)S(1)}, u32[]{:S(2)}, u32[]{:S(2)}) %collective-permute-start) | collective-permute-done | bytes 184352 | tf_op jit(solution)/shard_map/ppermute | solution.py:25
  26.3 2.6 %collective-permute-start.1 = (bf16[64,1440]{1,0:T(8,128)(2,1)S(1)}, bf16[64,1440]{1,0:T(8,128)(2,1)S(1)}, u32[]{:S(2)}, u32[]{:S(2)}) collective-permute-start(bf16[64,1440]{1,0:T(8,128)(2,1)S(1)} %fusion.4), channel_id=1, source_target_pairs={{0,16},{2,18},{4,20},{6,22},{8,24},{10,26},{12,28},{14,30},{16,0},... | collective-permute-start | bytes 552968 | tf_op jit(solution)/shard_map/ppermute | solution.py:25
  29.2 2.4 %collective-permute-start.4 = (bf16[1,40,1440]{2,1,0:T(8,128)(2,1)S(1)}, bf16[1,40,1440]{2,1,0:T(8,128)(2,1)S(1)}, u32[]{:S(2)}, u32[]{:S(2)}) collective-permute-start(bf16[1,40,1440]{2,1,0:T(8,128)(2,1)S(1)} %get-tuple-element.61), channel_id=1, source_target_pairs={{0,12},{2,14},{4,8},{6,10},{8,4},{10,6},{12,0},{14,2},{16,28},{18,... | collective-permute-start | bytes 345608 | tf_op jit(solution)/shard_map/ppermute | solution.py:25
  33.2 5.8 %collective-permute-done.4 = bf16[1,40,1440]{2,1,0:T(8,128)(2,1)S(1)} collective-permute-done((bf16[1,40,1440]{2,1,0:T(8,128)(2,1)S(1)}, bf16[1,40,1440]{2,1,0:T(8,128)(2,1)S(1)}, u32[]{:S(2)}, u32[]{:S(2)}) %collective-permute-start.4) | collective-permute-done | bytes 115232 | tf_op jit(solution)/shard_map/ppermute | solution.py:25
  40.5 1.5 %collective-permute-start.5 = (bf16[160,1440]{1,0:T(8,128)(2,1)S(1)}, bf16[160,1440]{1,0:T(8,128)(2,1)S(1)}, u32[]{:S(2)}, u32[]{:S(2)}) collective-permute-start(bf16[160,1440]{1,0:T(8,128)(2,1)S(1)} %constant_dynamic-update-slice_fusion.refs_0_), channel_id=1, source_target_pairs={{0,1},{1,0},{2,3},{3,2},{4,5},{5,4},{6,7},{7,6},{8,9},{9,8},{10,11... | collective-permute-start | bytes 1382408 | tf_op jit(solution)/shard_map/ppermute | solution.py:25
  43.2 13.2 %collective-permute-done.8 = bf16[64,1440]{1,0:T(8,128)(2,1)S(1)} collective-permute-done((bf16[64,1440]{1,0:T(8,128)(2,1)S(1)}, bf16[64,1440]{1,0:T(8,128)(2,1)S(1)}, u32[]{:S(2)}, u32[]{:S(2)}) %collective-permute-start.8) | collective-permute-done | bytes 184352 | tf_op jit(solution)/shard_map/ppermute | solution.py:25
  57.0 6.1 %collective-permute-done.9 = bf16[2,40,1440]{2,1,0:T(8,128)(2,1)S(1)} collective-permute-done((bf16[2,40,1440]{2,1,0:T(8,128)(2,1)S(1)}, bf16[2,40,1440]{2,1,0:T(8,128)(2,1)S(1)}, u32[]{:S(2)}, u32[]{:S(2)}) %collective-permute-start.9) | collective-permute-done | bytes 230432 | tf_op jit(solution)/shard_map/ppermute | solution.py:25
  64.9 5.9 %shard_map.148.refs_0_ = bf16[320,720]{1,0:T(8,128)(2,1)S(1)} custom-call(s32[1]{0:T(128)} %bitcast.me_ref, bf16[720,2880]{1,0:T(8,128)(2,1)} %bitcast.106, bf16[720,2880]{1,0:T(8,128)(2,1)} %bitcast.108, f32[1,2880]{1,0:T(1,128)} %reshape.155.gain_ref, bf16[160,1440]{1,0:T(8,128)(2,1)S(1)} %constant_dynamic-update-slice_fusion.refs_0_, ...), custom_call_target="tpu_custom_call" | custom-call | tf_op jit(solution)/shard_map/pallas_call | solution.py:224
  70.9 1.8 %collective-permute-done.12 = bf16[2,40,1440]{2,1,0:T(8,128)(2,1)S(1)} collective-permute-done((bf16[2,40,1440]{2,1,0:T(8,128)(2,1)S(1)}, bf16[2,40,1440]{2,1,0:T(8,128)(2,1)S(1)}, u32[]{:S(2)}, u32[]{:S(2)}) %collective-permute-start.12) | collective-permute-done | bytes 230432 | tf_op jit(solution)/shard_map/ppermute | solution.py:25
  72.7 3.4 %collective-permute-done.11 = bf16[2,40,1440]{2,1,0:T(8,128)(2,1)S(1)} collective-permute-done((bf16[2,40,1440]{2,1,0:T(8,128)(2,1)S(1)}, bf16[2,40,1440]{2,1,0:T(8,128)(2,1)S(1)}, u32[]{:S(2)}, u32[]{:S(2)}) %collective-permute-start.11) | collective-permute-done | bytes 230432 | tf_op jit(solution)/shard_map/ppermute | solution.py:25
  76.3 1.5 %collective-permute-start.14 = (bf16[320,720]{1,0:T(8,128)(2,1)S(1)}, bf16[320,720]{1,0:T(8,128)(2,1)S(1)}, u32[]{:S(2)}, u32[]{:S(2)}) collective-permute-start(bf16[320,720]{1,0:T(8,128)(2,1)S(1)} %shard_map.148.refs_0_), channel_id=1, source_target_pairs={{0,1},{1,0},{2,3},{3,2},{4,5},{5,4},{6,7},{7,6},{8,9},{9,8},{10,11... | collective-permute-start | bytes 1382408 | tf_op jit(solution)/shard_map/ppermute | solution.py:25
  78.9 6.1 %shard_map.149.refs_0_ = bf16[320,720]{1,0:T(8,128)(2,1)S(1)} custom-call(s32[1]{0:T(128)} %bitcast.me_ref, bf16[720,2880]{1,0:T(8,128)(2,1)} %bitcast.107, bf16[720,2880]{1,0:T(8,128)(2,1)} %bitcast.109, f32[1,2880]{1,0:T(1,128)} %reshape.155.gain_ref, bf16[2,160,1440]{2,1,0:T(8,128)(2,1)S(1)} %constant_dynamic-update-slice_fusion.4.refs_0_, ...), custom_call_target="tpu_custom_call" | custom-call | tf_op jit(solution)/shard_map/pallas_call | solution.py:224
  85.0 1.5 %collective-permute-start.19 = (bf16[320,720]{1,0:T(8,128)(2,1)S(1)}, bf16[320,720]{1,0:T(8,128)(2,1)S(1)}, u32[]{:S(2)}, u32[]{:S(2)}) collective-permute-start(bf16[320,720]{1,0:T(8,128)(2,1)S(1)} %shard_map.149.refs_0_), channel_id=1, source_target_pairs={{0,1},{1,0},{2,3},{3,2},{4,5},{5,4},{6,7},{7,6},{8,9},{9,8},{10,11... | collective-permute-start | bytes 1382408 | tf_op jit(solution)/shard_map/ppermute | solution.py:25
  86.6 3.9 %collective-permute-done.14.refs_1_ = bf16[320,720]{1,0:T(8,128)(2,1)S(1)} collective-permute-done((bf16[320,720]{1,0:T(8,128)(2,1)S(1)}, bf16[320,720]{1,0:T(8,128)(2,1)S(1)}, u32[]{:S(2)}, u32[]{:S(2)}) %collective-permute-start.14) | collective-permute-done | bytes 460832 | tf_op jit(solution)/shard_map/ppermute | solution.py:25
  90.4 3.5 %shard_map.150 = (bf16[160,1440]{1,0:T(8,128)(2,1)S(1)}, bf16[160,1440]{1,0:T(8,128)(2,1)S(1)}) custom-call(s32[1]{0:T(128)} %bitcast.me_ref, bf16[2,720,1440]{2,1,0:T(8,128)(2,1)} %bitcast.104, bf16[320,720]{1,0:T(8,128)(2,1)S(1)} %shard_map.148.refs_0_, bf16[320,720]{1,0:T(8,128)(2,1)S(1)} %collective-permute-done.14.refs_1_), custom_call_target="tpu_custom_call" | custom-call | tf_op jit(solution)/shard_map/pallas_call | solution.py:224
  94.3 6.2 %collective-permute-done.19.refs_1_ = bf16[320,720]{1,0:T(8,128)(2,1)S(1)} collective-permute-done((bf16[320,720]{1,0:T(8,128)(2,1)S(1)}, bf16[320,720]{1,0:T(8,128)(2,1)S(1)}, u32[]{:S(2)}, u32[]{:S(2)}) %collective-permute-start.19) | collective-permute-done | bytes 460832 | tf_op jit(solution)/shard_map/ppermute | solution.py:25
  100.5 3.5 %shard_map.151 = (bf16[160,1440]{1,0:T(8,128)(2,1)S(1)}, bf16[160,1440]{1,0:T(8,128)(2,1)S(1)}) custom-call(s32[1]{0:T(128)} %bitcast.me_ref, bf16[2,720,1440]{2,1,0:T(8,128)(2,1)} %bitcast.105, bf16[320,720]{1,0:T(8,128)(2,1)S(1)} %shard_map.149.refs_0_, bf16[320,720]{1,0:T(8,128)(2,1)S(1)} %collective-permute-done.19.refs_1_), custom_call_target="tpu_custom_call" | custom-call | tf_op jit(solution)/shard_map/pallas_call | solution.py:224
  104.2 1.7 %collective-permute-done.20 = bf16[160,1440]{1,0:T(8,128)(2,1)S(1)} collective-permute-done((bf16[160,1440]{1,0:T(8,128)(2,1)S(1)}, bf16[160,1440]{1,0:T(8,128)(2,1)S(1)}, u32[]{:S(2)}, u32[]{:S(2)}) %collective-permute-start.20) | collective-permute-done | bytes 460832 | tf_op jit(solution)/shard_map/ppermute | solution.py:25
  106.1 2.1 %collective-permute-start.21 = (bf16[40,1440]{1,0:T(8,128)(2,1)S(1)}, bf16[40,1440]{1,0:T(8,128)(2,1)S(1)}, u32[]{:S(2)}, u32[]{:S(2)}) collective-permute-start(bf16[40,1440]{1,0:T(8,128)(2,1)S(1)} %get-tuple-element.56), channel_id=1, source_target_pairs={{0,4},{2,6},{4,0},{6,2},{8,12},{10,14},{12,8},{14,10},{16,20},{18,... | collective-permute-start | bytes 345608 | tf_op jit(solution)/shard_map/ppermute | solution.py:25
  108.2 1.5 %collective-permute-start.23 = (bf16[40,1440]{1,0:T(8,128)(2,1)S(1)}, bf16[40,1440]{1,0:T(8,128)(2,1)S(1)}, u32[]{:S(2)}, u32[]{:S(2)}) collective-permute-start(bf16[40,1440]{1,0:T(8,128)(2,1)S(1)} %get-tuple-element.54), channel_id=1, source_target_pairs={{0,12},{2,14},{4,8},{6,10},{8,4},{10,6},{12,0},{14,2},{16,28},{18,... | collective-permute-start | bytes 345608 | tf_op jit(solution)/shard_map/ppermute | solution.py:25
  109.8 2.0 %collective-permute-start.16 = (bf16[40,1440]{1,0:T(8,128)(2,1)S(1)}, bf16[40,1440]{1,0:T(8,128)(2,1)S(1)}, u32[]{:S(2)}, u32[]{:S(2)}) collective-permute-start(bf16[40,1440]{1,0:T(8,128)(2,1)S(1)} %get-tuple-element.60), channel_id=1, source_target_pairs={{0,4},{2,6},{4,0},{6,2},{8,12},{10,14},{12,8},{14,10},{16,20},{18,... | collective-permute-start | bytes 345608 | tf_op jit(solution)/shard_map/ppermute | solution.py:25
  111.8 1.5 %collective-permute-start.18 = (bf16[40,1440]{1,0:T(8,128)(2,1)S(1)}, bf16[40,1440]{1,0:T(8,128)(2,1)S(1)}, u32[]{:S(2)}, u32[]{:S(2)}) collective-permute-start(bf16[40,1440]{1,0:T(8,128)(2,1)S(1)} %get-tuple-element.58), channel_id=1, source_target_pairs={{0,12},{2,14},{4,8},{6,10},{8,4},{10,6},{12,0},{14,2},{16,28},{18,... | collective-permute-start | bytes 345608 | tf_op jit(solution)/shard_map/ppermute | solution.py:25
  114.4 2.2 %collective-permute-done.23 = bf16[40,1440]{1,0:T(8,128)(2,1)S(1)} collective-permute-done((bf16[40,1440]{1,0:T(8,128)(2,1)S(1)}, bf16[40,1440]{1,0:T(8,128)(2,1)S(1)}, u32[]{:S(2)}, u32[]{:S(2)}) %collective-permute-start.23) | collective-permute-done | bytes 115232 | tf_op jit(solution)/shard_map/ppermute | solution.py:25
  117.0 2.2 %collective-permute-start.24 = (bf16[64,1440]{1,0:T(8,128)(2,1)S(1)}, bf16[64,1440]{1,0:T(8,128)(2,1)S(1)}, u32[]{:S(2)}, u32[]{:S(2)}) collective-permute-start(bf16[64,1440]{1,0:T(8,128)(2,1)S(1)} %fusion.3), channel_id=1, source_target_pairs={{0,16},{2,18},{4,20},{6,22},{8,24},{10,26},{12,28},{14,30},{16,0},... | collective-permute-start | bytes 552968 | tf_op jit(solution)/shard_map/ppermute | solution.py:25
  119.3 2.3 %collective-permute-done.17 = bf16[40,1440]{1,0:T(8,128)(2,1)S(1)} collective-permute-done((bf16[40,1440]{1,0:T(8,128)(2,1)S(1)}, bf16[40,1440]{1,0:T(8,128)(2,1)S(1)}, u32[]{:S(2)}, u32[]{:S(2)}) %collective-permute-start.17) | collective-permute-done | bytes 115232 | tf_op jit(solution)/shard_map/ppermute | solution.py:25
  121.5 1.7 %collective-permute-done.18 = bf16[40,1440]{1,0:T(8,128)(2,1)S(1)} collective-permute-done((bf16[40,1440]{1,0:T(8,128)(2,1)S(1)}, bf16[40,1440]{1,0:T(8,128)(2,1)S(1)}, u32[]{:S(2)}, u32[]{:S(2)}) %collective-permute-start.18) | collective-permute-done | bytes 115232 | tf_op jit(solution)/shard_map/ppermute | solution.py:25
  123.5 4.1 %collective-permute-done.24 = bf16[64,1440]{1,0:T(8,128)(2,1)S(1)} collective-permute-done((bf16[64,1440]{1,0:T(8,128)(2,1)S(1)}, bf16[64,1440]{1,0:T(8,128)(2,1)S(1)}, u32[]{:S(2)}, u32[]{:S(2)}) %collective-permute-start.24) | collective-permute-done | bytes 184352 | tf_op jit(solution)/shard_map/ppermute | solution.py:25
  (78 shorter events, 16.2 us)
Async XLA Ops:
  0.0 16.1 %all-to-all-start = ((bf16[16,8,512]{2,1,0:T(8,128)(2,1)}), bf16[16,8,512]{2,1,0:T(8,128)(2,1)S(1)}, u32[]{:S(2)}, u32[]{:S(2)}) async-start(bf16[16,8,512]{2,1,0:T(8,128)(2,1)} %bitcast.112), calls=%async_computation | async-start | bytes 262144 | tf_op jit(solution)/shard_map/all_to_all | solution.py:265
  11.2 0.7 copy-start
  19.0 7.3 %collective-permute-start = (bf16[64,1440]{1,0:T(8,128)(2,1)S(1)}, bf16[64,1440]{1,0:T(8,128)(2,1)S(1)}, u32[]{:S(2)}, u32[]{:S(2)}) collective-permute-start(bf16[64,1440]{1,0:T(8,128)(2,1)S(1)} %get-tuple-element.31), channel_id=1, source_target_pairs={{0,1},{1,0},{2,3},{3,2},{4,5},{5,4},{6,7},{7,6},{8,9},{9,8},{10,11... | collective-permute-start | bytes 552968 | tf_op jit(solution)/shard_map/ppermute | solution.py:25
  20.8 12.0 %copy-start.1 = (f32[64,4]{0,1:T(4,128)S(1)}, f32[64,4]{0,1:T(4,128)}, u32[]{:S(2)}) copy-start(f32[64,4]{0,1:T(4,128)} %param.26) | copy-start | bytes 3076
  26.3 12.8 %collective-permute-start.1 = (bf16[64,1440]{1,0:T(8,128)(2,1)S(1)}, bf16[64,1440]{1,0:T(8,128)(2,1)S(1)}, u32[]{:S(2)}, u32[]{:S(2)}) collective-permute-start(bf16[64,1440]{1,0:T(8,128)(2,1)S(1)} %fusion.4), channel_id=1, source_target_pairs={{0,16},{2,18},{4,20},{6,22},{8,24},{10,26},{12,28},{14,30},{16,0},... | collective-permute-start | bytes 552968 | tf_op jit(solution)/shard_map/ppermute | solution.py:25
  29.2 9.8 %collective-permute-start.4 = (bf16[1,40,1440]{2,1,0:T(8,128)(2,1)S(1)}, bf16[1,40,1440]{2,1,0:T(8,128)(2,1)S(1)}, u32[]{:S(2)}, u32[]{:S(2)}) collective-permute-start(bf16[1,40,1440]{2,1,0:T(8,128)(2,1)S(1)} %get-tuple-element.61), channel_id=1, source_target_pairs={{0,12},{2,14},{4,8},{6,10},{8,4},{10,6},{12,0},{14,2},{16,28},{18,... | collective-permute-start | bytes 345608 | tf_op jit(solution)/shard_map/ppermute | solution.py:25
  31.7 8.8 %collective-permute-start.3 = (bf16[1,40,1440]{2,1,0:T(8,128)(2,1)S(1)}, bf16[1,40,1440]{2,1,0:T(8,128)(2,1)S(1)}, u32[]{:S(2)}, u32[]{:S(2)}) collective-permute-start(bf16[1,40,1440]{2,1,0:T(8,128)(2,1)S(1)} %get-tuple-element.62), channel_id=1, source_target_pairs={{0,8},{2,10},{4,12},{6,14},{8,0},{10,2},{12,4},{14,6},{16,24},{18,... | collective-permute-start | bytes 345608 | tf_op jit(solution)/shard_map/ppermute | solution.py:25
  32.2 8.2 %collective-permute-start.2 = (bf16[1,40,1440]{2,1,0:T(8,128)(2,1)S(1)}, bf16[1,40,1440]{2,1,0:T(8,128)(2,1)S(1)}, u32[]{:S(2)}, u32[]{:S(2)}) collective-permute-start(bf16[1,40,1440]{2,1,0:T(8,128)(2,1)S(1)} %get-tuple-element.63), channel_id=1, source_target_pairs={{0,4},{2,6},{4,0},{6,2},{8,12},{10,14},{12,8},{14,10},{16,20},{18,... | collective-permute-start | bytes 345608 | tf_op jit(solution)/shard_map/ppermute | solution.py:25
  32.8 9.3 %collective-permute-start.7 = (f32[64,8]{0,1:T(8,128)S(1)}, f32[64,8]{0,1:T(8,128)S(1)}, u32[]{:S(2)}, u32[]{:S(2)}) collective-permute-start(f32[64,8]{0,1:T(8,128)S(1)} %pad_maximum_fusion.7), channel_id=1, source_target_pairs={{0,16},{2,18},{4,20},{6,22},{8,24},{10,26},{12,28},{14,30},{16,0},... | collective-permute-start | bytes 6152 | tf_op jit(solution)/shard_map/ppermute | solution.py:25
  40.5 22.5 %collective-permute-start.5 = (bf16[160,1440]{1,0:T(8,128)(2,1)S(1)}, bf16[160,1440]{1,0:T(8,128)(2,1)S(1)}, u32[]{:S(2)}, u32[]{:S(2)}) collective-permute-start(bf16[160,1440]{1,0:T(8,128)(2,1)S(1)} %constant_dynamic-update-slice_fusion.refs_0_), channel_id=1, source_target_pairs={{0,1},{1,0},{2,3},{3,2},{4,5},{5,4},{6,7},{7,6},{8,9},{9,8},{10,11... | collective-permute-start | bytes 1382408 | tf_op jit(solution)/shard_map/ppermute | solution.py:25
  42.3 14.1 %collective-permute-start.8 = (bf16[64,1440]{1,0:T(8,128)(2,1)S(1)}, bf16[64,1440]{1,0:T(8,128)(2,1)S(1)}, u32[]{:S(2)}, u32[]{:S(2)}) collective-permute-start(bf16[64,1440]{1,0:T(8,128)(2,1)S(1)} %collective-permute-done.1), channel_id=1, source_target_pairs={{0,1},{1,0},{2,3},{3,2},{4,5},{5,4},{6,7},{7,6},{8,9},{9,8},{10,11... | collective-permute-start | bytes 552968 | tf_op jit(solution)/shard_map/ppermute | solution.py:25
  56.8 6.3 %collective-permute-start.9 = (bf16[2,40,1440]{2,1,0:T(8,128)(2,1)S(1)}, bf16[2,40,1440]{2,1,0:T(8,128)(2,1)S(1)}, u32[]{:S(2)}, u32[]{:S(2)}) collective-permute-start(bf16[2,40,1440]{2,1,0:T(8,128)(2,1)S(1)} %get-tuple-element.50), channel_id=1, source_target_pairs={{0,4},{2,6},{4,0},{6,2},{8,12},{10,14},{12,8},{14,10},{16,20},{18,... | collective-permute-start | bytes 691208 | tf_op jit(solution)/shard_map/ppermute | solution.py:25
  56.9 7.7 %collective-permute-start.6 = (bf16[160,1440]{1,0:T(8,128)(2,1)S(1)}, bf16[160,1440]{1,0:T(8,128)(2,1)S(1)}, u32[]{:S(2)}, u32[]{:S(2)}) collective-permute-start(bf16[160,1440]{1,0:T(8,128)(2,1)S(1)} %constant_dynamic-update-slice_fusion.refs_0_), channel_id=1, source_target_pairs={{0,2},{2,0},{4,6},{6,4},{8,10},{10,8},{12,14},{14,12},{16,18},{18,... | collective-permute-start | bytes 1382408 | tf_op jit(solution)/shard_map/ppermute | solution.py:25
  63.1 1.9 %collective-permute-start.10 = (bf16[160,1440]{1,0:T(8,128)(2,1)S(1)}, bf16[160,1440]{1,0:T(8,128)(2,1)S(1)}, u32[]{:S(2)}, u32[]{:S(2)}) collective-permute-start(bf16[160,1440]{1,0:T(8,128)(2,1)S(1)} %collective-permute-done.5.refs_1_), channel_id=1, source_target_pairs={{0,2},{2,0},{4,6},{6,4},{8,10},{10,8},{12,14},{14,12},{16,18},{18,... | collective-permute-start | bytes 1382408 | tf_op jit(solution)/shard_map/ppermute | solution.py:25
  63.1 9.7 %collective-permute-start.12 = (bf16[2,40,1440]{2,1,0:T(8,128)(2,1)S(1)}, bf16[2,40,1440]{2,1,0:T(8,128)(2,1)S(1)}, u32[]{:S(2)}, u32[]{:S(2)}) collective-permute-start(bf16[2,40,1440]{2,1,0:T(8,128)(2,1)S(1)} %get-tuple-element.49), channel_id=1, source_target_pairs={{0,12},{2,14},{4,8},{6,10},{8,4},{10,6},{12,0},{14,2},{16,28},{18,... | collective-permute-start | bytes 691208 | tf_op jit(solution)/shard_map/ppermute | solution.py:25
  63.8 12.3 %collective-permute-start.11 = (bf16[2,40,1440]{2,1,0:T(8,128)(2,1)S(1)}, bf16[2,40,1440]{2,1,0:T(8,128)(2,1)S(1)}, u32[]{:S(2)}, u32[]{:S(2)}) collective-permute-start(bf16[2,40,1440]{2,1,0:T(8,128)(2,1)S(1)} %get-tuple-element.52), channel_id=1, source_target_pairs={{0,8},{2,10},{4,12},{6,14},{8,0},{10,2},{12,4},{14,6},{16,24},{18,... | collective-permute-start | bytes 691208 | tf_op jit(solution)/shard_map/ppermute | solution.py:25
  76.3 2.6 %collective-permute-start.13 = (bf16[2,160,1440]{2,1,0:T(8,128)(2,1)S(1)}, bf16[2,160,1440]{2,1,0:T(8,128)(2,1)S(1)}, u32[]{:S(2)}, u32[]{:S(2)}) collective-permute-start(bf16[2,160,1440]{2,1,0:T(8,128)(2,1)S(1)} %constant_dynamic-update-slice_fusion.4.refs_0_), channel_id=1, source_target_pairs={{0,2},{2,0},{4,6},{6,4},{8,10},{10,8},{12,14},{14,12},{16,18},{18,... | collective-permute-start | bytes 2764808 | tf_op jit(solution)/shard_map/ppermute | solution.py:25
  76.3 14.1 %collective-permute-start.14 = (bf16[320,720]{1,0:T(8,128)(2,1)S(1)}, bf16[320,720]{1,0:T(8,128)(2,1)S(1)}, u32[]{:S(2)}, u32[]{:S(2)}) collective-permute-start(bf16[320,720]{1,0:T(8,128)(2,1)S(1)} %shard_map.148.refs_0_), channel_id=1, source_target_pairs={{0,1},{1,0},{2,3},{3,2},{4,5},{5,4},{6,7},{7,6},{8,9},{9,8},{10,11... | collective-permute-start | bytes 1382408 | tf_op jit(solution)/shard_map/ppermute | solution.py:25
  85.0 15.5 %collective-permute-start.19 = (bf16[320,720]{1,0:T(8,128)(2,1)S(1)}, bf16[320,720]{1,0:T(8,128)(2,1)S(1)}, u32[]{:S(2)}, u32[]{:S(2)}) collective-permute-start(bf16[320,720]{1,0:T(8,128)(2,1)S(1)} %shard_map.149.refs_0_), channel_id=1, source_target_pairs={{0,1},{1,0},{2,3},{3,2},{4,5},{5,4},{6,7},{7,6},{8,9},{9,8},{10,11... | collective-permute-start | bytes 1382408 | tf_op jit(solution)/shard_map/ppermute | solution.py:25
  93.9 10.2 %collective-permute-start.15 = (bf16[160,1440]{1,0:T(8,128)(2,1)S(1)}, bf16[160,1440]{1,0:T(8,128)(2,1)S(1)}, u32[]{:S(2)}, u32[]{:S(2)}) collective-permute-start(bf16[160,1440]{1,0:T(8,128)(2,1)S(1)} %get-tuple-element.45), channel_id=1, source_target_pairs={{0,2},{2,0},{4,6},{6,4},{8,10},{10,8},{12,14},{14,12},{16,18},{18,... | collective-permute-start | bytes 1382408 | tf_op jit(solution)/shard_map/ppermute | solution.py:25
  104.0 1.9 %collective-permute-start.20 = (bf16[160,1440]{1,0:T(8,128)(2,1)S(1)}, bf16[160,1440]{1,0:T(8,128)(2,1)S(1)}, u32[]{:S(2)}, u32[]{:S(2)}) collective-permute-start(bf16[160,1440]{1,0:T(8,128)(2,1)S(1)} %get-tuple-element.48), channel_id=1, source_target_pairs={{0,2},{2,0},{4,6},{6,4},{8,10},{10,8},{12,14},{14,12},{16,18},{18,... | collective-permute-start | bytes 1382408 | tf_op jit(solution)/shard_map/ppermute | solution.py:25
  106.1 5.7 %collective-permute-start.21 = (bf16[40,1440]{1,0:T(8,128)(2,1)S(1)}, bf16[40,1440]{1,0:T(8,128)(2,1)S(1)}, u32[]{:S(2)}, u32[]{:S(2)}) collective-permute-start(bf16[40,1440]{1,0:T(8,128)(2,1)S(1)} %get-tuple-element.56), channel_id=1, source_target_pairs={{0,4},{2,6},{4,0},{6,2},{8,12},{10,14},{12,8},{14,10},{16,20},{18,... | collective-permute-start | bytes 345608 | tf_op jit(solution)/shard_map/ppermute | solution.py:25
  108.2 6.2 %collective-permute-start.22 = (bf16[40,1440]{1,0:T(8,128)(2,1)S(1)}, bf16[40,1440]{1,0:T(8,128)(2,1)S(1)}, u32[]{:S(2)}, u32[]{:S(2)}) collective-permute-start(bf16[40,1440]{1,0:T(8,128)(2,1)S(1)} %get-tuple-element.55), channel_id=1, source_target_pairs={{0,8},{2,10},{4,12},{6,14},{8,0},{10,2},{12,4},{14,6},{16,24},{18,... | collective-permute-start | bytes 345608 | tf_op jit(solution)/shard_map/ppermute | solution.py:25
  108.2 8.4 %collective-permute-start.23 = (bf16[40,1440]{1,0:T(8,128)(2,1)S(1)}, bf16[40,1440]{1,0:T(8,128)(2,1)S(1)}, u32[]{:S(2)}, u32[]{:S(2)}) collective-permute-start(bf16[40,1440]{1,0:T(8,128)(2,1)S(1)} %get-tuple-element.54), channel_id=1, source_target_pairs={{0,12},{2,14},{4,8},{6,10},{8,4},{10,6},{12,0},{14,2},{16,28},{18,... | collective-permute-start | bytes 345608 | tf_op jit(solution)/shard_map/ppermute | solution.py:25
  109.8 9.5 %collective-permute-start.16 = (bf16[40,1440]{1,0:T(8,128)(2,1)S(1)}, bf16[40,1440]{1,0:T(8,128)(2,1)S(1)}, u32[]{:S(2)}, u32[]{:S(2)}) collective-permute-start(bf16[40,1440]{1,0:T(8,128)(2,1)S(1)} %get-tuple-element.60), channel_id=1, source_target_pairs={{0,4},{2,6},{4,0},{6,2},{8,12},{10,14},{12,8},{14,10},{16,20},{18,... | collective-permute-start | bytes 345608 | tf_op jit(solution)/shard_map/ppermute | solution.py:25
  111.8 9.8 %collective-permute-start.17 = (bf16[40,1440]{1,0:T(8,128)(2,1)S(1)}, bf16[40,1440]{1,0:T(8,128)(2,1)S(1)}, u32[]{:S(2)}, u32[]{:S(2)}) collective-permute-start(bf16[40,1440]{1,0:T(8,128)(2,1)S(1)} %get-tuple-element.59), channel_id=1, source_target_pairs={{0,8},{2,10},{4,12},{6,14},{8,0},{10,2},{12,4},{14,6},{16,24},{18,... | collective-permute-start | bytes 345608 | tf_op jit(solution)/shard_map/ppermute | solution.py:25
  111.8 11.5 %collective-permute-start.18 = (bf16[40,1440]{1,0:T(8,128)(2,1)S(1)}, bf16[40,1440]{1,0:T(8,128)(2,1)S(1)}, u32[]{:S(2)}, u32[]{:S(2)}) collective-permute-start(bf16[40,1440]{1,0:T(8,128)(2,1)S(1)} %get-tuple-element.58), channel_id=1, source_target_pairs={{0,12},{2,14},{4,8},{6,10},{8,4},{10,6},{12,0},{14,2},{16,28},{18,... | collective-permute-start | bytes 345608 | tf_op jit(solution)/shard_map/ppermute | solution.py:25
  117.0 10.5 %collective-permute-start.24 = (bf16[64,1440]{1,0:T(8,128)(2,1)S(1)}, bf16[64,1440]{1,0:T(8,128)(2,1)S(1)}, u32[]{:S(2)}, u32[]{:S(2)}) collective-permute-start(bf16[64,1440]{1,0:T(8,128)(2,1)S(1)} %fusion.3), channel_id=1, source_target_pairs={{0,16},{2,18},{4,20},{6,22},{8,24},{10,26},{12,28},{14,30},{16,0},... | collective-permute-start | bytes 552968 | tf_op jit(solution)/shard_map/ppermute | solution.py:25
